TPU v7x, 128 devices: a whole 4x4x4 slice. The times are simulated.
128 devices in a mesh: gx: 8 (over z_lo, y), gy: 16 (over z_hi, x, core).
Axes of the slice: x: 4, y: 4, z: 4 (z_hi: 2, z_lo: 2; z = z_hi * 2 + z_lo), core: 2. Of those that a mesh axis runs over, the one named last changes fastest.
Arguments:
- adjoint_prev: float32 [2, 20, 512, 2048], P(None, None, 'gx', 'gy'), may hold values from -2 to 2
- viscosity: float32 [20, 512, 2048], P(None, 'gx', 'gy'), may hold values from 0.5 to 4
- friction: float32 [512, 2048], P('gx', 'gy'), may hold values from 0.5 to 20
- basal_velocity: float32 [2, 512, 2048], P(None, 'gx', 'gy'), may hold values from -6 to 6
- ice_mask: int32 [512, 2048], P('gx', 'gy'), may hold values 0 or 1
- misfit: bfloat16 [131072, 2, 128], P(('gx', 'gy')), may hold values from -60 to 60
- block_tile: int32 [131072, 1], P(('gx', 'gy')), may hold values from 0 to 127; in each aligned block of 1024 rows (0 to 1023, 1024 to 2047, ...) at most 16 rows name the same one
- block_row: int32 [131072], P(('gx', 'gy')), may hold values from 0 to 63
Outputs:
- adjoint: float32 [2, 20, 512, 2048], P(None, None, 'gx', 'gy')
- gradient: float32 [512, 2048], P('gx', 'gy')
Inputs may be any that keep to these rules, and one draw needn't show every extreme that they name: `block_tile`: among the 1024 blocks of one device no tile is named more than 16 times, a bound that some block reaches.
All inputs are finite; a program needn't handle non-finite values. No bound on the sum of `ice_mask` on one device may be relied on, other than what follows from the above.
Results may differ from a plain program's by a relative error of at most 0.0003.
Values may be sent and summed in bfloat16 or wider, within the bound.
A program may use at most 64 MiB of HBM per device.

v0:
```python
import math

import jax
import jax.numpy as jnp
from jax import lax
from jax.sharding import PartitionSpec as P

ITERS = 3


VERTICAL = 4.0


def with_halo(array, sides, width):
    for axis, dim in sides:
        peers, length = (lax.axis_size(axis), array.shape[dim])
        up = [(i, (i + 1) % peers) for i in range(peers - 1)]
        down = [(j, i) for i, j in up]
        last = lax.slice_in_dim(array, length - width, length, axis=dim)
        initial = lax.slice_in_dim(array, 0, width, axis=dim)
        before = lax.ppermute(last, axis, up)
        after = lax.ppermute(initial, axis, down)
        array = jnp.concatenate([before, array, after], axis=dim)
    return array


def omega_list(count):
    return [
        1.0 / (1.3 + 1.2 * math.cos((2 * turn_id + 1) * math.pi / (2 * count)))
        for turn_id in range(count)
    ]


def coefficients(padded_eta, friction):
    center = padded_eta[:, 1:-1, 1:-1]
    x_low = 0.5 * (padded_eta[:, :-2, 1:-1] + center)
    x_high = 0.5 * (padded_eta[:, 2:, 1:-1] + center)
    y_low = 0.5 * (padded_eta[:, 1:-1, :-2] + center)
    y_high = 0.5 * (padded_eta[:, 1:-1, 2:] + center)
    layer_face = 0.5 * (center[:-1] + center[1:])
    zero_face = jnp.zeros_like(center[:1])
    z_up = jnp.concatenate([zero_face, layer_face], axis=0)
    z_down = jnp.concatenate([layer_face, zero_face], axis=0)
    basal = jnp.concatenate([jnp.zeros_like(center[:-1]), friction[None]], axis=0)
    horiz_x = x_low + x_high
    horiz_y = y_low + y_high
    vertical = VERTICAL * (z_up + z_down) + basal
    diagonal = jnp.stack([4.0 * horiz_x + horiz_y + vertical, horiz_x + 4.0 * horiz_y + vertical])
    return ((x_low, x_high, y_low, y_high, z_up, z_down, basal), diagonal)


def diffuse(padded, coeff, weight_x, weight_y):
    x_low, x_high, y_low, y_high, z_up, z_down, basal = coeff
    center = padded[:, 1:-1, 1:-1]
    zero_layer = jnp.zeros_like(center[:1])
    above = jnp.concatenate([zero_layer, center[:-1]], axis=0)
    below = jnp.concatenate([center[1:], zero_layer], axis=0)
    total = weight_x * (
        x_low * (center - padded[:, :-2, 1:-1]) + x_high * (center - padded[:, 2:, 1:-1])
    )
    total = total + weight_y * (
        y_low * (center - padded[:, 1:-1, :-2]) + y_high * (center - padded[:, 1:-1, 2:])
    )
    total = total + VERTICAL * (z_up * (center - above) + z_down * (center - below))
    return total + basal * center


def mixed(padded, padded_eta, weight_x, weight_y):
    along_y = 0.5 * (padded[:, :, 2:] - padded[:, :, :-2])
    flux_x = weight_x * padded_eta[:, :, 1:-1] * along_y
    along_x = 0.5 * (padded[:, 2:, :] - padded[:, :-2, :])
    flux_y = weight_y * padded_eta[:, 1:-1, :] * along_x
    return -(0.5 * (flux_x[:, 2:] - flux_x[:, :-2]) + 0.5 * (flux_y[:, :, 2:] - flux_y[:, :, :-2]))


def operate(padded_adj, padded_eta, coeff):
    first = diffuse(padded_adj[0], coeff, 4.0, 1.0) + mixed(padded_adj[1], padded_eta, 2.0, 1.0)
    second = diffuse(padded_adj[1], coeff, 1.0, 4.0) + mixed(padded_adj[0], padded_eta, 1.0, 2.0)
    return jnp.stack([first, second])


def extend(stacked):
    return with_halo(stacked, (("gx", 1), ("gy", 2)), 1)


def on_device(
    adjoint_prev, viscosity, friction, basal_velocity, ice_mask, misfit, block_tile, block_row
):
    count_x = lax.axis_size("gx")
    count_y = lax.axis_size("gy")
    device_count = count_x * count_y
    block_count = misfit.shape[0]
    tile_cols = misfit.shape[2]
    capacity = 2 * block_count // device_count
    layer_count = adjoint_prev.shape[1]
    tile_rows = adjoint_prev.shape[2]
    target = block_tile[:, 0]
    onehot = (target[:, None] == jnp.arange(device_count, dtype=jnp.int32)[None, :]).astype(
        jnp.int32
    )
    before = jnp.cumsum(onehot, axis=0) - onehot
    position = jnp.sum(before * onehot, axis=1)
    slot_id = target * capacity + position
    slot_total = device_count * capacity
    slot_block = math.gcd(slot_total, 512)
    flat_misfit = misfit.reshape(block_count, 2 * tile_cols)

    def pack_slots(first_slot):
        wanted = first_slot + jnp.arange(slot_block, dtype=jnp.int32)
        select = wanted[:, None] == slot_id[None, :]
        picked = jnp.dot(
            select.astype(jnp.bfloat16), flat_misfit, preferred_element_type=jnp.float32
        )
        filled = jnp.any(select, axis=1)
        rows_here = jnp.sum(jnp.where(select, block_row[None, :], 0), axis=1)
        rows_here = jnp.where(filled, rows_here, -1)
        return (picked.astype(jnp.bfloat16), rows_here)

    starts = jnp.arange(slot_total // slot_block, dtype=jnp.int32) * slot_block
    packed_values, packed_rows = lax.map(pack_slots, starts)
    send_values = packed_values.reshape(slot_total, 2, tile_cols)
    send_rows = packed_rows.reshape(slot_total)
    got_values, got_rows = (
        lax.all_to_all(
            send_values.reshape(device_count, capacity, 2, tile_cols),
            ("gx", "gy"),
            split_axis=0,
            concat_axis=0,
            tiled=True,
        ),
        lax.all_to_all(
            send_rows.reshape(device_count, capacity),
            ("gx", "gy"),
            split_axis=0,
            concat_axis=0,
            tiled=True,
        ),
    )
    got_values = got_values.reshape(device_count * capacity, 2, tile_cols)
    got_rows = got_rows.reshape(device_count * capacity)
    row_table = (got_rows[:, None] == jnp.arange(tile_rows, dtype=jnp.int32)[None, :]).astype(
        jnp.bfloat16
    )
    surface = jnp.einsum("rx,rcy->cxy", row_table, got_values, preferred_element_type=jnp.float32)
    ice = ice_mask.astype(jnp.float32)
    adjoint = ice * adjoint_prev
    source = jnp.zeros(adjoint_prev.shape, jnp.float32).at[:, 0].set(surface)
    padded_eta = None
    coeff = None
    diagonal = None
    for turn_id, omega in enumerate(omega_list(ITERS)):
        flat_adjoint = adjoint.reshape(2 * layer_count, tile_rows, tile_cols)
        if turn_id == 0:
            padded = extend(jnp.concatenate([flat_adjoint, viscosity], axis=0))
            padded_adj = padded[: 2 * layer_count]
            padded_eta = padded[2 * layer_count :]
            coeff, diagonal = coefficients(padded_eta, friction)
        else:
            padded_adj = extend(flat_adjoint)
        padded_adj = padded_adj.reshape(2, layer_count, tile_rows + 2, tile_cols + 2)
        image = operate(padded_adj, padded_eta, coeff)
        adjoint = ice * (adjoint + omega * (source - image) / diagonal)
    gradient = (
        -friction
        * ice
        * (
            basal_velocity[0] * adjoint[0, layer_count - 1]
            + basal_velocity[1] * adjoint[1, layer_count - 1]
        )
    )
    return (adjoint, gradient)


def solution(mesh):
    placed = (
        P(None, None, "gx", "gy"),
        P(None, "gx", "gy"),
        P("gx", "gy"),
        P(None, "gx", "gy"),
        P("gx", "gy"),
        P(("gx", "gy"), None, None),
        P(("gx", "gy"), None),
        P(("gx", "gy")),
    )
    return jax.shard_map(
        on_device,
        mesh=mesh,
        in_specs=placed,
        out_specs=(P(None, None, "gx", "gy"), P("gx", "gy")),
        check_vma=False,
    )
```

profile of v0, /device:TPU:31, one launch (start us, length us, event | category | flops | bytes accessed | tf_op | source)
XLA Modules:
  0.0 182.8 jit_solution(15910266000612799012)
XLA Ops:
  3.0 3.2 %collective-permute-start = (f32[60,1,128]{2,1,0:T(1,128)S(1)}, f32[60,1,128]{2,1,0:T(1,128)S(1)}, u32[]{:S(2)}, u32[]{:S(2)}) collective-permute-start(f32[60,1,128]{2,1,0:T(1,128)S(1)} %get-tuple-element.97), channel_id=1, source_target_pairs={{0,16},{16,32},{32,48},{48,64},{64,80},{80,96},{96,112},{1,17},{17... | collective-permute-start | bytes 92168 | tf_op jit(solution)/shard_map/ppermute | solution.py:21
  6.2 2.1 %collective-permute-start.1 = (f32[60,1,128]{2,1,0:T(1,128)S(1)}, f32[60,1,128]{2,1,0:T(1,128)S(1)}, u32[]{:S(2)}, u32[]{:S(2)}) collective-permute-start(f32[60,1,128]{2,1,0:T(1,128)S(1)} %get-tuple-element.98), channel_id=1, source_target_pairs={{16,0},{32,16},{48,32},{64,48},{80,64},{96,80},{112,96},{17,1},{33... | collective-permute-start | bytes 92168 | tf_op jit(solution)/shard_map/ppermute | solution.py:22
  9.8 12.6 %while.13 = (s32[]{:T(128)}, bf16[4,512,256]{2,1,0:T(8,128)(2,1)}, s32[4,512]{1,0:T(4,128)S(1)}, s32[4]{0:T(128)S(1)}, s32[1024]{0:T(1024)S(1)}, /*index=5*/bf16...) while((s32[]{:T(128)}, bf16[4,512,256]{2,1,0:T(8,128)(2,1)}, s32[4,512]{1,0:T(4,128)S(1)}, ...), condition=%wide.region_6.7_spmd, body=%wide.region_3.0_spmd.sunk | while | flops 271712256 | bytes 822897 | solution.py:120
  23.1 11.6 %all-to-all-start.1 = ((s32[128,1,16]{2,1,0:T(1,128)}), s32[128,1,16]{2,1,0:T(1,128)}, u32[]{:S(2)}, u32[]{:S(2)}) async-start(s32[128,1,16]{2,1,0:T(1,128)} %bitcast.9), calls=%async_computation.1 | async-start | bytes 131072 | tf_op jit(solution)/shard_map/all_to_all | solution.py:131
  37.1 2.1 %fusion.167 = (f32[60,66,1]{2,1,0:T(8,128)}, f32[60,66,1]{2,1,0:T(8,128)S(1)}) fusion(f32[60,66,128]{2,1,0:T(8,128)S(1)} %pad_maximum_fusion.3), kind=kLoop, calls=%fused_computation.281 | loop fusion | bytes 63360 | tf_op jit(solution)/shard_map/slice | solution.py:19
  39.2 3.0 %copy.117 = f32[60,66,1]{1,2,0:T(1,128)} copy(f32[60,66,1]{2,1,0:T(8,128)} %get-tuple-element.95) | data formatting | bytes 31680 | tf_op jit(solution)/shard_map/slice | solution.py:19
  42.1 5.3 %collective-permute-start.2 = (f32[60,66,1]{1,2,0:T(1,128)}, f32[60,66,1]{1,2,0:T(1,128)}, u32[]{:S(2)}, u32[]{:S(2)}) collective-permute-start(f32[60,66,1]{1,2,0:T(1,128)} %copy.117), channel_id=1, source_target_pairs={{0,1},{1,2},{2,3},{3,4},{4,5},{5,6},{6,7},{7,8},{8,9},{9,10},{10,1... | collective-permute-start | bytes 47528 | tf_op jit(solution)/shard_map/ppermute | solution.py:21
  48.8 2.0 %collective-permute-start.3 = (f32[60,66,1]{1,2,0:T(1,128)}, f32[60,66,1]{1,2,0:T(1,128)}, u32[]{:S(2)}, u32[]{:S(2)}) collective-permute-start(f32[60,66,1]{1,2,0:T(1,128)} %copy.119), channel_id=1, source_target_pairs={{1,0},{2,1},{3,2},{4,3},{5,4},{6,5},{7,6},{8,7},{9,8},{10,9},{11,1... | collective-permute-start | bytes 47528 | tf_op jit(solution)/shard_map/ppermute | solution.py:22
  53.6 9.7 %all-to-all-start = ((bf16[128,16,2,128]{3,1,2,0:T(8,128)(2,1)}), bf16[128,16,2,128]{3,1,2,0:T(8,128)(2,1)}, u32[]{:S(2)}, u32[]{:S(2)}) async-start(bf16[128,16,2,128]{3,1,2,0:T(8,128)(2,1)} %copy.114), calls=%async_computation | async-start | bytes 2097152 | tf_op jit(solution)/shard_map/all_to_all | solution.py:124
  67.7 2.9 %copy.120 = f32[60,66,1]{2,1,0:T(8,128)} copy(f32[60,66,1]{1,2,0:T(1,128)} %collective-permute-done.3) | data formatting | bytes 31680 | tf_op jit(solution)/shard_map/ppermute | solution.py:22
  70.6 5.5 %pad_maximum_fusion = f32[60,66,130]{2,1,0:T(8,128)S(1)} fusion(f32[60,66,1]{2,1,0:T(8,128)} %copy.120, f32[60,1,128]{2,1,0:T(1,128)} %copy-done.49, f32[20,64,128]{2,1,0:T(8,128)} %param.13, f32[40,64,128]{2,1,0:T(8,128)S(1)} %bitcast.118, f32[60,1,128]{2,1,0:T(1,128)S(1)} %collective-permute-done, f32[60,66,1]{2,1,0:T(8,128)S(1)} %copy.118), kind=kLoop, calls=%fused_computation.12 | loop fusion | flops 2574000 | bytes 4118400 | tf_op jit(solution)/shard_map/concatenate | solution.py:23
  81.7 4.5 %fusion.53 = (f32[1,20,64,128]{3,2,1,0:T(8,128)}, f32[20,64,128]{2,1,0:T(8,128)S(1)}, f32[20,64,128]{2,1,0:T(8,128)S(1)}, f32[20,64,128]{2,1,0:T(8,128)S(1)}, f32[20,64,128]{2,1,0:T(8,128)S(1)}) fusion(f32[1,64,128]{2,1,0:T(8,128)S(1)} %bitcast.138, f32[20,64,130]{2,1,0:T(8,128)S(1)} %get-tuple-element.92, f32[20,66,128]{2,1,0:T(8,128)S(1)} %fusion.50, ...), kind=kLoop, calls=%fused_computation.101 | loop fusion | flops 9666560 | bytes 10513344 | tf_op jit(solution)/shard_map/stack | solution.py:79
  88.6 3.0 %fusion.56 = f32[1,20,64,128]{3,2,1,0:T(8,128)} fusion(f32[1,64,128]{2,1,0:T(8,128)S(1)} %bitcast.140, f32[20,64,130]{2,1,0:T(8,128)S(1)} %get-tuple-element.91, f32[20,66,128]{2,1,0:T(8,128)S(1)} %fusion.48, f32[20,64,128]{2,1,0:T(8,128)S(1)} %get-tuple-element.81, f32[60,66,1]{2,1,0:T(8,128)S(1)} %copy-done, f32[60,1,128]{2,1,0:T(1,128)S(1)} %copy-done.50, ...), kind=kLoop, calls=%fused_computation.104 | loop fusion | flops 6389760 | bytes 10513344 | tf_op jit(solution)/shard_map/stack | solution.py:79
  95.4 3.2 %collective-permute-start.4 = (f32[40,1,128]{2,1,0:T(1,128)S(1)}, f32[40,1,128]{2,1,0:T(1,128)S(1)}, u32[]{:S(2)}, u32[]{:S(2)}) collective-permute-start(f32[40,1,128]{2,1,0:T(1,128)S(1)} %get-tuple-element.113), channel_id=1, source_target_pairs={{0,16},{16,32},{32,48},{48,64},{64,80},{80,96},{96,112},{1,17},{17... | collective-permute-start | bytes 61448 | tf_op jit(solution)/shard_map/ppermute | solution.py:21
  98.5 2.1 %collective-permute-start.5 = (f32[40,1,128]{2,1,0:T(1,128)S(1)}, f32[40,1,128]{2,1,0:T(1,128)S(1)}, u32[]{:S(2)}, u32[]{:S(2)}) collective-permute-start(f32[40,1,128]{2,1,0:T(1,128)S(1)} %get-tuple-element.114), channel_id=1, source_target_pairs={{16,0},{32,16},{48,32},{64,48},{80,64},{96,80},{112,96},{17,1},{33... | collective-permute-start | bytes 61448 | tf_op jit(solution)/shard_map/ppermute | solution.py:22
  101.8 3.3 %collective-permute-done.5 = f32[40,1,128]{2,1,0:T(1,128)S(1)} collective-permute-done((f32[40,1,128]{2,1,0:T(1,128)S(1)}, f32[40,1,128]{2,1,0:T(1,128)S(1)}, u32[]{:S(2)}, u32[]{:S(2)}) %collective-permute-start.5) | collective-permute-done | bytes 20512 | tf_op jit(solution)/shard_map/ppermute | solution.py:22
  108.9 6.5 %collective-permute-start.6 = (f32[40,66,1]{1,0,2:T(8,128)S(1)}, f32[40,66,1]{1,0,2:T(8,128)S(1)}, u32[]{:S(2)}, u32[]{:S(2)}) collective-permute-start(f32[40,66,1]{1,0,2:T(8,128)S(1)} %copy.125), channel_id=1, source_target_pairs={{0,1},{1,2},{2,3},{3,4},{4,5},{5,6},{6,7},{7,8},{8,9},{9,10},{10,1... | collective-permute-start | bytes 31688 | tf_op jit(solution)/shard_map/ppermute | solution.py:21
  115.9 2.1 %collective-permute-start.7 = (f32[40,66,1]{1,0,2:T(8,128)S(1)}, f32[40,66,1]{1,0,2:T(8,128)S(1)}, u32[]{:S(2)}, u32[]{:S(2)}) collective-permute-start(f32[40,66,1]{1,0,2:T(8,128)S(1)} %copy.127), channel_id=1, source_target_pairs={{1,0},{2,1},{3,2},{4,3},{5,4},{6,5},{7,6},{8,7},{9,8},{10,9},{11,1... | collective-permute-start | bytes 31688 | tf_op jit(solution)/shard_map/ppermute | solution.py:22
  119.8 4.7 %collective-permute-done.7 = f32[40,66,1]{1,0,2:T(8,128)S(1)} collective-permute-done((f32[40,66,1]{1,0,2:T(8,128)S(1)}, f32[40,66,1]{1,0,2:T(8,128)S(1)}, u32[]{:S(2)}, u32[]{:S(2)}) %collective-permute-start.7) | collective-permute-done | bytes 10592 | tf_op jit(solution)/shard_map/ppermute | solution.py:22
  126.3 2.7 %pad_maximum_fusion.1 = f32[40,66,130]{2,1,0:T(8,128)S(1)} fusion(f32[40,66,1]{2,1,0:T(8,128)} %copy.128, f32[40,1,128]{2,1,0:T(1,128)S(1)} %collective-permute-done.5, f32[40,64,128]{2,1,0:T(8,128)S(1)} %bitcast.126, f32[40,1,128]{2,1,0:T(1,128)S(1)} %collective-permute-done.4, f32[40,66,1]{2,1,0:T(8,128)S(1)} %copy.126), kind=kLoop, calls=%fused_computation.13 | loop fusion | flops 1372800 | bytes 2745600 | tf_op jit(solution)/shard_map/concatenate | solution.py:23
  129.1 2.1 %fusion.21 = (f32[20,64,130]{2,1,0:T(8,128)S(1)}, f32[20,64,130]{2,1,0:T(8,128)S(1)}) fusion(f32[40,66,130]{2,1,0:T(8,128)S(1)} %pad_maximum_fusion.1, f32[60,66,130]{2,1,0:T(8,128)} %copy-done.3), kind=kLoop, calls=%fused_computation.36 | loop fusion | flops 1164800 | bytes 4659200 | tf_op jit(solution)/shard_map/mul | solution.py:72
  131.2 3.2 %fusion.45 = (f32[20,66,128]{2,1,0:T(8,128)S(1)}, f32[20,66,128]{2,1,0:T(8,128)S(1)}) fusion(f32[40,66,1]{2,1,0:T(8,128)} %copy-done.10, f32[40,1,128]{2,1,0:T(1,128)S(1)} %collective-permute-done.5, f32[40,64,128]{2,1,0:T(8,128)S(1)} %bitcast.127, f32[40,1,128]{2,1,0:T(1,128)S(1)} %collective-permute-done.4, f32[40,66,1]{2,1,0:T(8,128)S(1)} %copy-done.12, ...), kind=kLoop, calls=%fused_computation.84 | loop fusion | flops 3210240 | bytes 3400320 | tf_op jit(solution)/shard_map/mul | solution.py:70
  142.9 3.4 %collective-permute-start.9 = (f32[40,1,128]{2,1,0:T(1,128)S(1)}, f32[40,1,128]{2,1,0:T(1,128)S(1)}, u32[]{:S(2)}, u32[]{:S(2)}) collective-permute-start(f32[40,1,128]{2,1,0:T(1,128)S(1)} %get-tuple-element.106), channel_id=1, source_target_pairs={{16,0},{32,16},{48,32},{64,48},{80,64},{96,80},{112,96},{17,1},{33... | collective-permute-start | bytes 61448 | tf_op jit(solution)/shard_map/ppermute | solution.py:22
  147.1 2.4 %collective-permute-done.9 = f32[40,1,128]{2,1,0:T(1,128)S(1)} collective-permute-done((f32[40,1,128]{2,1,0:T(1,128)S(1)}, f32[40,1,128]{2,1,0:T(1,128)S(1)}, u32[]{:S(2)}, u32[]{:S(2)}) %collective-permute-start.9) | collective-permute-done | bytes 20512 | tf_op jit(solution)/shard_map/ppermute | solution.py:22
  149.7 2.0 %fusion.168 = (f32[40,66,1]{2,1,0:T(8,128)}, f32[40,66,1]{2,1,0:T(8,128)}) fusion(f32[40,66,128]{2,1,0:T(8,128)S(1)} %pad_maximum_fusion.5), kind=kLoop, calls=%fused_computation.282 | loop fusion | bytes 42240 | tf_op jit(solution)/shard_map/slice | solution.py:19
  153.6 3.7 %collective-permute-start.10 = (f32[40,66,1]{1,0,2:T(8,128)S(1)}, f32[40,66,1]{1,0,2:T(8,128)S(1)}, u32[]{:S(2)}, u32[]{:S(2)}) collective-permute-start(f32[40,66,1]{1,0,2:T(8,128)S(1)} %copy.135), channel_id=1, source_target_pairs={{0,1},{1,2},{2,3},{3,4},{4,5},{5,6},{6,7},{7,8},{8,9},{9,10},{10,1... | collective-permute-start | bytes 31688 | tf_op jit(solution)/shard_map/ppermute | solution.py:21
  159.2 2.2 %collective-permute-start.11 = (f32[40,66,1]{1,0,2:T(8,128)S(1)}, f32[40,66,1]{1,0,2:T(8,128)S(1)}, u32[]{:S(2)}, u32[]{:S(2)}) collective-permute-start(f32[40,66,1]{1,0,2:T(8,128)S(1)} %copy.137), channel_id=1, source_target_pairs={{1,0},{2,1},{3,2},{4,3},{5,4},{6,5},{7,6},{8,7},{9,8},{10,9},{11,1... | collective-permute-start | bytes 31688 | tf_op jit(solution)/shard_map/ppermute | solution.py:22
  161.4 2.0 %slice_bitcast_fusion.6 = f32[19,64,128]{2,1,0:T(8,128)} fusion(f32[2,20,64,128]{3,2,0,1:T(8,128)} %copy-done.25), kind=kLoop, calls=%fused_computation.250 | loop fusion | bytes 1245184 | tf_op jit(solution)/shard_map/slice | solution.py:57
  165.1 2.9 %collective-permute-done.11 = f32[40,66,1]{1,0,2:T(8,128)S(1)} collective-permute-done((f32[40,66,1]{1,0,2:T(8,128)S(1)}, f32[40,66,1]{1,0,2:T(8,128)S(1)}, u32[]{:S(2)}, u32[]{:S(2)}) %collective-permute-start.11) | collective-permute-done | bytes 10592 | tf_op jit(solution)/shard_map/ppermute | solution.py:22
  169.7 3.2 %pad_maximum_fusion.2 = f32[40,66,130]{2,1,0:T(8,128)S(1)} fusion(f32[40,66,1]{2,1,0:T(8,128)} %copy.138, f32[40,1,128]{2,1,0:T(1,128)S(1)} %collective-permute-done.9, f32[40,64,128]{2,1,0:T(8,128)S(1)} %bitcast.133, f32[40,1,128]{2,1,0:T(1,128)S(1)} %collective-permute-done.8, f32[40,66,1]{2,1,0:T(8,128)} %copy.136), kind=kLoop, calls=%fused_computation.14 | loop fusion | flops 1372800 | bytes 2745600 | tf_op jit(solution)/shard_map/concatenate | solution.py:23
  172.9 2.1 %fusion.17 = (f32[20,64,130]{2,1,0:T(8,128)S(1)}, f32[20,64,130]{2,1,0:T(8,128)S(1)}) fusion(f32[40,66,130]{2,1,0:T(8,128)S(1)} %pad_maximum_fusion.2, f32[60,66,130]{2,1,0:T(8,128)} %copy-done.3), kind=kLoop, calls=%fused_computation.30 | loop fusion | flops 1164800 | bytes 4659200 | tf_op jit(solution)/shard_map/mul | solution.py:72
  175.2 2.7 %fusion.40 = (f32[20,66,128]{2,1,0:T(8,128)S(1)}, f32[20,66,128]{2,1,0:T(8,128)S(1)}) fusion(f32[40,66,1]{2,1,0:T(8,128)S(1)} %copy-done.8, f32[40,1,128]{2,1,0:T(1,128)S(1)} %collective-permute-done.9, f32[40,64,128]{2,1,0:T(8,128)S(1)} %bitcast.134, f32[40,1,128]{2,1,0:T(1,128)S(1)} %collective-permute-done.8, f32[40,66,1]{2,1,0:T(8,128)S(1)} %copy-done.9, ...), kind=kLoop, calls=%fused_computation.72 | loop fusion | flops 3210240 | bytes 3400320 | tf_op jit(solution)/shard_map/mul | solution.py:70
  (216 shorter events, 69.8 us)
Async XLA Ops:
  2.9 5.4 %copy-start.56 = (s32[1024,1]{0,1:T(1,128)S(1)}, s32[1024,1]{0,1:T(1,128)}, u32[]{:S(2)}) copy-start(s32[1024,1]{0,1:T(1,128)} %param.18) | copy-start | bytes 12292
  3.0 33.2 %collective-permute-start = (f32[60,1,128]{2,1,0:T(1,128)S(1)}, f32[60,1,128]{2,1,0:T(1,128)S(1)}, u32[]{:S(2)}, u32[]{:S(2)}) collective-permute-start(f32[60,1,128]{2,1,0:T(1,128)S(1)} %get-tuple-element.97), channel_id=1, source_target_pairs={{0,16},{16,32},{32,48},{48,64},{64,80},{80,96},{96,112},{1,17},{17... | collective-permute-start | bytes 92168 | tf_op jit(solution)/shard_map/ppermute | solution.py:21
  6.2 30.0 %collective-permute-start.1 = (f32[60,1,128]{2,1,0:T(1,128)S(1)}, f32[60,1,128]{2,1,0:T(1,128)S(1)}, u32[]{:S(2)}, u32[]{:S(2)}) collective-permute-start(f32[60,1,128]{2,1,0:T(1,128)S(1)} %get-tuple-element.98), channel_id=1, source_target_pairs={{16,0},{32,16},{48,32},{64,48},{80,64},{96,80},{112,96},{17,1},{33... | collective-permute-start | bytes 92168 | tf_op jit(solution)/shard_map/ppermute | solution.py:22
  23.1 30.5 %all-to-all-start.1 = ((s32[128,1,16]{2,1,0:T(1,128)}), s32[128,1,16]{2,1,0:T(1,128)}, u32[]{:S(2)}, u32[]{:S(2)}) async-start(s32[128,1,16]{2,1,0:T(1,128)} %bitcast.9), calls=%async_computation.1 | async-start | bytes 131072 | tf_op jit(solution)/shard_map/all_to_all | solution.py:131
  36.1 34.4 %copy-start.47 = (f32[60,1,128]{2,1,0:T(1,128)}, f32[60,1,128]{2,1,0:T(1,128)S(1)}, u32[]{:S(2)}) copy-start(f32[60,1,128]{2,1,0:T(1,128)S(1)} %collective-permute-done) | copy-start | bytes 92164
  42.1 23.9 %collective-permute-start.2 = (f32[60,66,1]{1,2,0:T(1,128)}, f32[60,66,1]{1,2,0:T(1,128)}, u32[]{:S(2)}, u32[]{:S(2)}) collective-permute-start(f32[60,66,1]{1,2,0:T(1,128)} %copy.117), channel_id=1, source_target_pairs={{0,1},{1,2},{2,3},{3,4},{4,5},{5,6},{6,7},{7,8},{8,9},{9,10},{10,1... | collective-permute-start | bytes 47528 | tf_op jit(solution)/shard_map/ppermute | solution.py:21
  48.8 3.3 %copy-start.51 = (bf16[4,512,256]{2,1,0:T(8,128)(2,1)S(1)}, bf16[4,512,256]{2,1,0:T(8,128)(2,1)}, u32[]{:S(2)}) copy-start(bf16[4,512,256]{2,1,0:T(8,128)(2,1)} %get-tuple-element.52) | copy-start | bytes 3145732
  48.8 18.9 %collective-permute-start.3 = (f32[60,66,1]{1,2,0:T(1,128)}, f32[60,66,1]{1,2,0:T(1,128)}, u32[]{:S(2)}, u32[]{:S(2)}) collective-permute-start(f32[60,66,1]{1,2,0:T(1,128)} %copy.119), channel_id=1, source_target_pairs={{1,0},{2,1},{3,2},{4,3},{5,4},{6,5},{7,6},{8,7},{9,8},{10,9},{11,1... | collective-permute-start | bytes 47528 | tf_op jit(solution)/shard_map/ppermute | solution.py:22
  53.6 38.0 %all-to-all-start = ((bf16[128,16,2,128]{3,1,2,0:T(8,128)(2,1)}), bf16[128,16,2,128]{3,1,2,0:T(8,128)(2,1)}, u32[]{:S(2)}, u32[]{:S(2)}) async-start(bf16[128,16,2,128]{3,1,2,0:T(8,128)(2,1)} %copy.114), calls=%async_computation | async-start | bytes 2097152 | tf_op jit(solution)/shard_map/all_to_all | solution.py:124
  76.1 3.2 %copy-start = (f32[60,66,1]{2,1,0:T(8,128)S(1)}, f32[60,66,1]{2,1,0:T(8,128)}, u32[]{:S(2)}) copy-start(f32[60,66,1]{2,1,0:T(8,128)} %copy.120) | copy-start | bytes 47524
  76.1 3.3 %copy-start.2 = (f32[20,64,128]{2,1,0:T(8,128)S(1)}, f32[20,64,128]{2,1,0:T(8,128)}, u32[]{:S(2)}) copy-start(f32[20,64,128]{2,1,0:T(8,128)} %param.13) | copy-start | bytes 1966084
  76.1 4.1 %copy-start.5 = (f32[60,66,128]{2,1,0:T(8,128)S(1)}, f32[60,66,128]{2,1,0:T(8,128)}, u32[]{:S(2)}) copy-start(f32[60,66,128]{2,1,0:T(8,128)} %copy-done.4) | copy-start | bytes 6082564
  76.1 4.1 %copy-start.48 = (f32[60,1,128]{2,1,0:T(1,128)S(1)}, f32[60,1,128]{2,1,0:T(1,128)}, u32[]{:S(2)}) copy-start(f32[60,1,128]{2,1,0:T(1,128)} %copy-done.47) | copy-start | bytes 92164
  76.2 4.0 %copy-start.50 = (f32[60,1,128]{2,1,0:T(1,128)S(1)}, f32[60,1,128]{2,1,0:T(1,128)}, u32[]{:S(2)}) copy-start(f32[60,1,128]{2,1,0:T(1,128)} %copy-done.49) | copy-start | bytes 92164
  95.4 6.5 %collective-permute-start.4 = (f32[40,1,128]{2,1,0:T(1,128)S(1)}, f32[40,1,128]{2,1,0:T(1,128)S(1)}, u32[]{:S(2)}, u32[]{:S(2)}) collective-permute-start(f32[40,1,128]{2,1,0:T(1,128)S(1)} %get-tuple-element.113), channel_id=1, source_target_pairs={{0,16},{16,32},{32,48},{48,64},{64,80},{80,96},{96,112},{1,17},{17... | collective-permute-start | bytes 61448 | tf_op jit(solution)/shard_map/ppermute | solution.py:21
  98.5 6.6 %collective-permute-start.5 = (f32[40,1,128]{2,1,0:T(1,128)S(1)}, f32[40,1,128]{2,1,0:T(1,128)S(1)}, u32[]{:S(2)}, u32[]{:S(2)}) collective-permute-start(f32[40,1,128]{2,1,0:T(1,128)S(1)} %get-tuple-element.114), channel_id=1, source_target_pairs={{16,0},{32,16},{48,32},{64,48},{80,64},{96,80},{112,96},{17,1},{33... | collective-permute-start | bytes 61448 | tf_op jit(solution)/shard_map/ppermute | solution.py:22
  108.9 10.4 %collective-permute-start.6 = (f32[40,66,1]{1,0,2:T(8,128)S(1)}, f32[40,66,1]{1,0,2:T(8,128)S(1)}, u32[]{:S(2)}, u32[]{:S(2)}) collective-permute-start(f32[40,66,1]{1,0,2:T(8,128)S(1)} %copy.125), channel_id=1, source_target_pairs={{0,1},{1,2},{2,3},{3,4},{4,5},{5,6},{6,7},{7,8},{8,9},{9,10},{10,1... | collective-permute-start | bytes 31688 | tf_op jit(solution)/shard_map/ppermute | solution.py:21
  115.9 8.7 %collective-permute-start.7 = (f32[40,66,1]{1,0,2:T(8,128)S(1)}, f32[40,66,1]{1,0,2:T(8,128)S(1)}, u32[]{:S(2)}, u32[]{:S(2)}) collective-permute-start(f32[40,66,1]{1,0,2:T(8,128)S(1)} %copy.127), channel_id=1, source_target_pairs={{1,0},{2,1},{3,2},{4,3},{5,4},{6,5},{7,6},{8,7},{9,8},{10,9},{11,1... | collective-permute-start | bytes 31688 | tf_op jit(solution)/shard_map/ppermute | solution.py:22
  119.8 9.2 %copy-start.10 = (f32[40,66,1]{2,1,0:T(8,128)}, f32[40,66,1]{2,1,0:T(8,128)S(1)}, u32[]{:S(2)}) copy-start(f32[40,66,1]{2,1,0:T(8,128)S(1)} %copy.126) | copy-start | bytes 31684
  131.2 3.2 %copy-start.7 = (f32[19,64,128]{2,1,0:T(8,128)S(1)}, f32[19,64,128]{2,1,0:T(8,128)}, u32[]{:S(2)}) copy-start(f32[19,64,128]{2,1,0:T(8,128)} %get-tuple-element.119) | copy-start | bytes 1867780
  131.2 3.2 %copy-start.11 = (f32[40,66,1]{2,1,0:T(8,128)S(1)}, f32[40,66,1]{2,1,0:T(8,128)}, u32[]{:S(2)}) copy-start(f32[40,66,1]{2,1,0:T(8,128)} %copy-done.10) | copy-start | bytes 31684
  131.2 3.2 %copy-start.14 = (f32[20,64,128]{2,1,0:T(8,128)S(1)}, f32[20,64,128]{2,1,0:T(8,128)}, u32[]{:S(2)}) copy-start(f32[20,64,128]{2,1,0:T(8,128)} %copy-done.13) | copy-start | bytes 1966084
  131.2 3.2 %copy-start.17 = (f32[20,64,128]{2,1,0:T(8,128)S(1)}, f32[20,64,128]{2,1,0:T(8,128)}, u32[]{:S(2)}) copy-start(f32[20,64,128]{2,1,0:T(8,128)} %copy-done.16) | copy-start | bytes 1966084
  131.2 3.2 %copy-start.20 = (f32[20,64,128]{2,1,0:T(8,128)S(1)}, f32[20,64,128]{2,1,0:T(8,128)}, u32[]{:S(2)}) copy-start(f32[20,64,128]{2,1,0:T(8,128)} %copy-done.19) | copy-start | bytes 1966084
  131.2 3.2 %copy-start.23 = (f32[20,64,128]{2,1,0:T(8,128)S(1)}, f32[20,64,128]{2,1,0:T(8,128)}, u32[]{:S(2)}) copy-start(f32[20,64,128]{2,1,0:T(8,128)} %copy-done.22) | copy-start | bytes 1966084
  131.2 3.2 %copy-start.37 = (f32[19,64,128]{2,1,0:T(8,128)S(1)}, f32[19,64,128]{2,1,0:T(8,128)}, u32[]{:S(2)}) copy-start(f32[19,64,128]{2,1,0:T(8,128)} %get-tuple-element.109) | copy-start | bytes 1867780
  131.2 3.3 %copy-start.38 = (f32[19,64,128]{2,1,0:T(8,128)S(1)}, f32[19,64,128]{2,1,0:T(8,128)}, u32[]{:S(2)}) copy-start(f32[19,64,128]{2,1,0:T(8,128)} %get-tuple-element.110) | copy-start | bytes 1867780
  141.0 6.2 %collective-permute-start.8 = (f32[40,1,128]{2,1,0:T(1,128)S(1)}, f32[40,1,128]{2,1,0:T(1,128)S(1)}, u32[]{:S(2)}, u32[]{:S(2)}) collective-permute-start(f32[40,1,128]{2,1,0:T(1,128)S(1)} %get-tuple-element.105), channel_id=1, source_target_pairs={{0,16},{16,32},{32,48},{48,64},{64,80},{80,96},{96,112},{1,17},{17... | collective-permute-start | bytes 61448 | tf_op jit(solution)/shard_map/ppermute | solution.py:21
  142.9 6.6 %collective-permute-start.9 = (f32[40,1,128]{2,1,0:T(1,128)S(1)}, f32[40,1,128]{2,1,0:T(1,128)S(1)}, u32[]{:S(2)}, u32[]{:S(2)}) collective-permute-start(f32[40,1,128]{2,1,0:T(1,128)S(1)} %get-tuple-element.106), channel_id=1, source_target_pairs={{16,0},{32,16},{48,32},{64,48},{80,64},{96,80},{112,96},{17,1},{33... | collective-permute-start | bytes 61448 | tf_op jit(solution)/shard_map/ppermute | solution.py:22
  153.6 9.8 %collective-permute-start.10 = (f32[40,66,1]{1,0,2:T(8,128)S(1)}, f32[40,66,1]{1,0,2:T(8,128)S(1)}, u32[]{:S(2)}, u32[]{:S(2)}) collective-permute-start(f32[40,66,1]{1,0,2:T(8,128)S(1)} %copy.135), channel_id=1, source_target_pairs={{0,1},{1,2},{2,3},{3,4},{4,5},{5,6},{6,7},{7,8},{8,9},{9,10},{10,1... | collective-permute-start | bytes 31688 | tf_op jit(solution)/shard_map/ppermute | solution.py:21
  159.2 8.7 %collective-permute-start.11 = (f32[40,66,1]{1,0,2:T(8,128)S(1)}, f32[40,66,1]{1,0,2:T(8,128)S(1)}, u32[]{:S(2)}, u32[]{:S(2)}) collective-permute-start(f32[40,66,1]{1,0,2:T(8,128)S(1)} %copy.137), channel_id=1, source_target_pairs={{1,0},{2,1},{3,2},{4,3},{5,4},{6,5},{7,6},{8,7},{9,8},{10,9},{11,1... | collective-permute-start | bytes 31688 | tf_op jit(solution)/shard_map/ppermute | solution.py:22
  175.1 2.8 %copy-start.33 = (f32[19,64,128]{2,1,0:T(8,128)S(1)}, f32[19,64,128]{2,1,0:T(8,128)}, u32[]{:S(2)}) copy-start(f32[19,64,128]{2,1,0:T(8,128)} %get-tuple-element.103) | copy-start | bytes 1867780
  (40 other events, 69.3 us)
where the time goes:
time: 184 us; the launch traced here: 183 us
  starting transfers between devices  59 us (32%)
  other arithmetic  54.6 us (30%)
  local copies, waits for them, and re-layouts  49.1 us (27%)
  waiting for transfers between devices  13.3 us (7%)
  matrix products  5.1 us (3%)
    ppermute x6, starting transfers between devices, with_halo(): before = lax.ppermute(last, axis, up)  23.8 us
    ppermute x6, starting transfers between devices, with_halo(): after = lax.ppermute(initial, axis, down)  13.9 us
    ppermute x6, waiting for transfers between devices, with_halo(): after = lax.ppermute(initial, axis, down)  13.3 us
    slice x8, local copies, waits for them, and re-layouts, with_halo(): last = lax.slice_in_dim(array, length - width, length, axis=dim)  12.5 us
    another operation x6, other arithmetic, operate(): return jnp.stack([first, second])  12.5 us
    concatenate x6, other arithmetic, with_halo(): array = jnp.concatenate([before, array, after], axis=dim)  12.1 us
    all_to_all x1, starting transfers between devices, on_device(): lax.all_to_all(send_rows.reshape(device_count, capacity), ('gx', 'gy'), s...  11.6 us
    all_to_all x1, starting transfers between devices, on_device(): lax.all_to_all(send_values.reshape(device_count, capacity, 2, tile_cols),...  9.72 us
  transfers between devices with their start and end apart: 14, of which 4 were waited for; matrix products, arithmetic and copies ran while one was open for 32% of the time, Pallas kernels for 0%

commit v1 on v0

v1 whole, which is shorter than its diff:
```python
import functools
import math

import jax
import jax.numpy as jnp
from jax import lax
from jax.experimental import pallas as pl
from jax.experimental.pallas import tpu as pltpu
from jax.sharding import PartitionSpec as P

ITERS = 3
GX = 8
GY = 16
TILES = GX * GY
CAP = 16
SB = 1024
LAYERS = 20
TX = 64
TY = 128
BASE = 16
ROWS = 96
F32 = jnp.float32
BF16 = jnp.bfloat16
MESH = pl.DeviceIdType.MESH
SIDES = ((0, -1), (0, 1), (-1, 0), (1, 0), (-1, -1), (-1, 1), (1, -1), (1, 1))


def omega_list(count):
    return [1.0 / (1.3 + 1.2 * math.cos((2 * k + 1) * math.pi / (2 * count))) for k in range(count)]


def lanes():
    return lax.broadcasted_iota(jnp.int32, (8, 128), 1)


def roll(x, shift):
    return pltpu.roll(x, shift, 1)


def four_n(e, f, o, heavy_x):
    exm, exp_, eym, eyp = e
    fxm, fxp, fym, fyp = f
    dym, dyp, dxm, dxp = o
    if heavy_x:
        x = exm * (4.0 * fxm - dym) + exp_ * (4.0 * fxp + dyp)
        y = eym * (2.0 * fym - dxm) + eyp * (2.0 * fyp + dxp)
        return 2.0 * x + y, 8.0 * (fxm + fxp), 2.0 * (fym + fyp)
    x = exm * (2.0 * fxm - dym) + exp_ * (2.0 * fxp + dyp)
    y = eym * (4.0 * fym - dxm) + eyp * (4.0 * fyp + dxp)
    return x + 2.0 * y, 2.0 * (fxm + fxp), 8.0 * (fym + fyp)


def kernel(
    adj_hbm, eta_hbm, fric_hbm, ice_hbm, mis_hbm, tile_hbm, row_hbm,
    out_ref, c3_ref,
    fa, fb, et, eym, eyp, gu, gv, icef, frip,
    e_own, e_left, e_right, pr, rr, s0, s1, s2, se, sg, ymv, ypv,
    tile_v, row_v, slot_v, mis_v, mis_f, vals, sendb, recvb, rsend, rrecv, surf,
    c1, c2, ec, tc1, tc2, te, tg, ycm, ycp,
    in_sem, a_send, a_recv, r_send, r_recv, h_send, h_recv, q_send, q_recv, c_send, c_recv, bar2,
):
    me_x = lax.axis_index("gx")
    me_y = lax.axis_index("gy")
    me = me_x * GY + me_y
    omegas = omega_list(ITERS)

    def at(dx, dy):
        return (lax.rem(me_x + dx + GX, GX), lax.rem(me_y + dy + GY, GY))

    ins = [
        (tile_hbm, tile_v), (row_hbm, row_v), (mis_hbm, mis_v),
        (ice_hbm, icef.at[pl.ds(BASE, TX)]), (fric_hbm, frip.at[pl.ds(BASE, TX)]),
        (eta_hbm, et.at[pl.ds(1, LAYERS), pl.ds(BASE, TX)]),
        (adj_hbm, fa.at[:, pl.ds(1, LAYERS), pl.ds(BASE, TX)]),
    ]
    loads = [pltpu.make_async_copy(s, d, in_sem.at[i]) for i, (s, d) in enumerate(ins)]
    for c in loads:
        c.start()
    barrier = pltpu.get_barrier_semaphore()
    for k in range(1, GY):
        pl.semaphore_signal(barrier, inc=1, device_id=at(0, k), device_id_type=MESH)
    for k in range(1, GX):
        pl.semaphore_signal(barrier, inc=1, device_id=at(k, 0), device_id_type=MESH)

    loads[0].wait()
    loads[1].wait()
    ii = lax.broadcasted_iota(jnp.int32, (256, 512), 0)
    jj = lax.broadcasted_iota(jnp.int32, (256, 512), 1)
    tri = jnp.where((ii < jj) | (jj >= 256), 1.0, 0.0).astype(BF16)
    tsub = lax.broadcasted_iota(jnp.int32, (TILES, 256), 0)
    running = jnp.zeros((TILES, 256), F32)
    rmat = jnp.zeros((TILES, 128), F32)
    for c in range(4):
        t = tile_v[:, pl.ds(256 * c, 256)]
        hit = jnp.where(t == tsub, 1.0, 0.0)
        hot = hit.astype(BF16)
        sums = jnp.dot(hot, tri, preferred_element_type=F32)
        pos = jnp.sum(hit * (running + sums[:, :256]), axis=0, keepdims=True)
        running = running + sums[:, 256:]
        slot_v[:, pl.ds(256 * c, 256)] = t.astype(F32) * float(CAP) + pos
        z = jnp.where(
            pos == (tsub & (CAP - 1)).astype(F32), row_v[:, pl.ds(256 * c, 256)].astype(F32) + 1.0, 0.0
        ).astype(BF16)
        rmat = rmat + lax.dot_general(hot, z, (((1,), (1,)), ((), ())), preferred_element_type=F32)
    rsend[...] = rmat.reshape(TILES, 1, 128)

    pl.semaphore_wait(barrier, GX + GY - 2)
    for k in range(1, GX):
        pl.semaphore_signal(bar2, inc=1, device_id=at(k, 0), device_id_type=MESH)

    for c in loads[3:]:
        c.wait()
    lane = lanes()

    def build(rb, carry):
        r = pl.multiple_of(BASE + rb * 8, 8)
        q = pl.multiple_of(8 + rb * 8, 8)
        ice = icef[pl.ds(r, 8)]
        edge = jnp.zeros((8, 128), F32)

        def put(acc, x, unit):
            return jnp.where((lane >= 8 * unit) & (lane < 8 * unit + 8), roll(x, (8 * unit + 4) % 128), acc)

        for kind in range(3):
            acc = jnp.zeros((8, 128), F32)
            for l in range(LAYERS):
                if kind < 2:
                    x = ice * fa[kind, l + 1, pl.ds(r, 8)]
                    fa[kind, l + 1, pl.ds(r, 8)] = x
                else:
                    x = et[l + 1, pl.ds(r, 8)]
                if l < 16:
                    acc = put(acc, x, l)
                else:
                    edge = put(edge, x, 4 * kind + l - 16)
            e_own[kind, pl.ds(q, 8)] = acc
        edge = put(edge, ice, 12)
        edge = put(edge, frip[pl.ds(r, 8)], 13)
        e_own[3, pl.ds(q, 8)] = edge
        return carry

    lax.fori_loop(0, 8, build, 0)

    def pack_rows(l, carry):
        for up in range(2):
            r = BASE + (TX - 4) * up
            pr[up, l] = fa[0, l + 1, pl.ds(r, 4)]
            pr[up, LAYERS + l] = fa[1, l + 1, pl.ds(r, 4)]
            pr[up, 2 * LAYERS + l] = et[l + 1, pl.ds(r, 4)]
        return carry

    lax.fori_loop(0, LAYERS, pack_rows, 0)
    for up in range(2):
        r = BASE + (TX - 4) * up
        pr[up, 3 * LAYERS] = icef[pl.ds(r, 4)]
        pr[up, 3 * LAYERS + 1] = frip[pl.ds(r, 4)]

    pl.semaphore_wait(bar2, GX - 1)

    def span(dx):
        if dx == 0:
            return pl.ds(8, TX), pl.ds(8, TX)
        return (pl.ds(8, 8), pl.ds(72, 8)) if dx < 0 else (pl.ds(64, 8), pl.ds(0, 8))

    halos = []
    for i, (dx, dy) in enumerate(SIDES):
        src, dst = span(dx)
        land = (e_right, e_own, e_left)[dy + 1]
        halos.append(
            pltpu.make_async_remote_copy(
                e_own.at[:, src], land.at[:, dst], h_send.at[i], h_recv.at[i],
                device_id=at(dx, dy), device_id_type=MESH,
            )
        )
    for up, dx in ((0, -1), (1, 1)):
        halos.append(
            pltpu.make_async_remote_copy(
                pr.at[up], rr.at[1 - up], q_send.at[up], q_recv.at[up], device_id=at(dx, 0), device_id_type=MESH
            )
        )
    for c in halos:
        c.start()

    loads[2].wait()

    def widen(i, carry):
        mis_f[pl.ds(pl.multiple_of(i * 128, 128), 128)] = mis_v[pl.ds(pl.multiple_of(i * 128, 128), 128)].astype(F32)
        return carry

    lax.fori_loop(0, 16, widen, 0)
    for c in range(2):
        for i in range(8):
            vals[pl.ds(128 * i, 128), pl.ds(128 * c, 128)] = mis_f[pl.ds(256 * i + c, 128, stride=2)].astype(BF16)

    own_values = pltpu.make_async_copy(sendb.at[me], recvb.at[me], a_recv.at[0])
    own_rows = pltpu.make_async_copy(rsend.at[me], rrecv.at[me], r_recv.at[0])
    own_rows.start()

    def pack(j, carry):
        px = lax.rem(me_x + j, GX)
        want = (px * (GY * CAP)).astype(F32) + lax.broadcasted_iota(jnp.int32, (256, SB), 0).astype(F32)
        sel = jnp.where(slot_v[...] == want, 1.0, 0.0).astype(BF16)
        got = jnp.dot(sel, vals[...], preferred_element_type=F32).astype(BF16)
        sendb[pl.ds(px * GY, GY)] = got.reshape(GY, CAP, 2 * TY)

        def send(k, inner):
            py = lax.rem(me_y + k, GY)
            d = px * GY + py
            pltpu.make_async_remote_copy(
                sendb.at[d], recvb.at[me], a_send, a_recv.at[j], device_id=(px, py), device_id_type=MESH
            ).start()
            pltpu.make_async_remote_copy(
                rsend.at[d], rrecv.at[me], r_send, r_recv.at[j], device_id=(px, py), device_id_type=MESH
            ).start()
            return inner

        lax.fori_loop(jnp.where(j == 0, 1, 0), GY, send, 0)
        return carry

    lax.fori_loop(0, GX, pack, 0)
    own_values.start()

    zero = jnp.zeros((8, 128), F32)

    def clear(r, carry):
        q = pl.ds(pl.multiple_of(r * 8, 8), 8)
        for end in (0, LAYERS + 1):
            et[end, q] = zero
            for c in range(2):
                fa[c, end, q] = zero
                fb[c, end, q] = zero
        return carry

    lax.fori_loop(0, ROWS // 8, clear, 0)

    def flag(cond):
        return jnp.where(cond, 1.0, 0.0).astype(F32)

    has_up, has_down = flag(me_x > 0), flag(me_x < GX - 1)
    has_left, has_right = flag(me_y > 0), flag(me_y < GY - 1)
    for c in halos:
        c.wait()

    def unpack_rows(l, carry):
        for side, r, has in ((0, BASE - 4, has_up), (1, BASE + TX, has_down)):
            fa[0, l + 1, pl.ds(r, 4)] = rr[side, l] * has
            fa[1, l + 1, pl.ds(r, 4)] = rr[side, LAYERS + l] * has
            et[l + 1, pl.ds(r, 4)] = rr[side, 2 * LAYERS + l] * has
        return carry

    lax.fori_loop(0, LAYERS, unpack_rows, 0)
    for side, r, has in ((0, BASE - 4, has_up), (1, BASE + TX, has_down)):
        icef[pl.ds(r, 4)] = rr[side, 3 * LAYERS] * has
        frip[pl.ds(r, 4)] = rr[side, 3 * LAYERS + 1] * has

    low4 = (lane & 7) < 4

    def tile_units(x):
        x = jnp.where(lane < 8, x, 0.0)
        for s in (8, 16, 32, 64):
            x = x + roll(x, s)
        return x

    for b in range(10):
        q = pl.ds(8 * b, 8)
        w = pl.ds(8 + 8 * b, 8)
        has = has_up if b == 0 else (has_down if b == 9 else 1.0)
        for side in range(2):
            parts = []
            for kind in range(4):
                own = e_own[kind, q] * has
                if side == 0:
                    parts.append(jnp.where(low4, own, e_right[kind, q] * (has * has_right)))
                else:
                    parts.append(jnp.where(low4, e_left[kind, q] * (has * has_left), own))
            mixed = parts[3]
            first = lane < 32
            s0[0, side, 0, w] = parts[0]
            s0[1, side, 0, w] = parts[1]
            se[side, 0, w] = parts[2]
            s0[0, side, 1, w] = jnp.where(first, mixed, 0.0)
            s0[1, side, 1, w] = jnp.where(first, roll(mixed, 96), 0.0)
            se[side, 1, w] = jnp.where(first, roll(mixed, 64), 0.0)
            sg[side, 0, w] = tile_units(roll(mixed, 32))
            sg[side, 1, w] = jnp.where((lane >= 24) & first, roll(mixed, 48), 0.0)

    def inverse(dx4, dy4, rest, ice):
        du = 4.0 * dx4 + dy4 + rest
        dv = dx4 + 4.0 * dy4 + rest
        live = ice > 0.0
        r = jnp.where(live, 0.25, 0.0) / jnp.where(live, du * dv, 1.0)
        return r * dv, r * du

    def neighbours(x_a, x_b, group):
        if group == 0:
            return (jnp.where(lane < 8, 0.0, roll(x_a, 8)), jnp.where(lane < 120, roll(x_a, 120), roll(x_b, 120)))
        return jnp.where(lane < 8, roll(x_a, 8), roll(x_b, 8)), roll(x_b, 120)

    starts = [14 + 8 * b for b in range(9)]

    def strip_inverse(side, carry):
        for r in starts:
            w = pl.ds(r, 8)
            ice = sg[side, 0, w]
            fric = sg[side, 1, w]
            ea, eb = se[side, 0, w], se[side, 1, w]
            for g, e in ((0, ea), (1, eb)):
                up, down = neighbours(ea, eb, g)
                live = ice if g == 0 else jnp.where(lane < 32, ice, 0.0)
                count = jnp.where((lane < 8) if g == 0 else (lane >= 24), 1.0, 2.0)
                dx4 = 0.5 * (se[side, g, pl.ds(r - 1, 8)] + se[side, g, pl.ds(r + 1, 8)]) + e
                dy4 = 0.5 * (roll(e, 1) + roll(e, 127)) + e
                rest = 2.0 * (up + down + count * e)
                if g == 1:
                    rest = rest + fric
                a, b = inverse(dx4, dy4, rest, live)
                sg[side, 2 + 2 * g, w] = a
                sg[side, 3 + 2 * g, w] = b
        return carry

    lax.fori_loop(0, 2, strip_inverse, 0)

    def shifted(x, left, right):
        return roll(jnp.where(lane == 127, left, x), 1), roll(jnp.where(lane == 0, right, x), 127)

    def main_inverse(l, carry):
        g = l // 16
        unit = l - 16 * g
        lroll, rroll = 124 - 8 * unit, 124 - 8 * unit
        bottom = flag(l == LAYERS - 1)
        count = 2.0 - flag(l == 0) - bottom
        for r in starts:
            w = pl.ds(r, 8)
            e = et[l + 1, w]
            ym, yp = shifted(e, roll(se[1, g, w], lroll), roll(se[0, g, w], rroll))
            eym[l, w] = ym
            eyp[l, w] = yp
            dx4 = 0.5 * (et[l + 1, pl.ds(r - 1, 8)] + et[l + 1, pl.ds(r + 1, 8)]) + e
            dy4 = 0.5 * (ym + yp) + e
            rest = 2.0 * (et[l, w] + et[l + 2, w] + count * e) + bottom * frip[w]
            a, b = inverse(dx4, dy4, rest, icef[w])
            gu[l, w] = a
            gv[l, w] = b
        return carry

    lax.fori_loop(0, LAYERS, main_inverse, 0)

    def strip_sweep(src, dst, omega):
        def one(side, carry):
            for r in starts:
                w, wm, wp = pl.ds(r, 8), pl.ds(r - 1, 8), pl.ds(r + 1, 8)
                ea, eb = se[side, 0, w], se[side, 1, w]
                both = [(src[c, side, 0, w], src[c, side, 1, w]) for c in range(2)]
                for g, e in ((0, ea), (1, eb)):
                    eu, ed = neighbours(ea, eb, g)
                    faces = (se[side, g, wm], se[side, g, wp], roll(e, 1), roll(e, 127))
                    own, diffs = [], []
                    for c in range(2):
                        m, z, p = src[c, side, g, wm], both[c][g], src[c, side, g, wp]
                        own.append((m, p, roll(z, 1), roll(z, 127)))
                        dx = p - m
                        diffs.append((roll(m, 127) - roll(m, 1), roll(p, 127) - roll(p, 1), roll(dx, 1), roll(dx, 127)))
                    for c in range(2):
                        up, down = neighbours(both[c][0], both[c][1], g)
                        total, nx, ny = four_n(faces, own[c], diffs[1 - c], c == 0)
                        total = total + e * (nx + ny + 8.0 * (up + down)) + 8.0 * (eu * up + ed * down)
                        dst[c, side, g, w] = (1.0 - omega) * both[c][g] + omega * (sg[side, 2 + 2 * g + c, w] * total)
            return carry

        lax.fori_loop(0, 2, one, 0)

    def main_sweep(src, strips, omega, rows_at, store):
        def one(l, carry):
            g = l // 16
            unit = l - 16 * g
            lroll, rroll = 124 - 8 * unit, 124 - 8 * unit
            for b in range(1, 11):
                w = pl.ds(8 * b, 8)
                for c in range(2):
                    ym, yp = shifted(
                        src[c, l + 1, w], roll(strips[c, 1, g, w], lroll), roll(strips[c, 0, g, w], rroll)
                    )
                    ymv[c, w] = ym
                    ypv[c, w] = yp
            for r in rows_at:
                w, wm, wp = pl.ds(r, 8), pl.ds(r - 1, 8), pl.ds(r + 1, 8)
                e, eu, ed = et[l + 1, w], et[l, w], et[l + 2, w]
                faces = (et[l + 1, wm], et[l + 1, wp], eym[l, w], eyp[l, w])
                own, diffs = [], []
                for c in range(2):
                    own.append((src[c, l + 1, wm], src[c, l + 1, wp], ymv[c, w], ypv[c, w]))
                    mm, mp, pm, pp = ymv[c, wm], ypv[c, wm], ymv[c, wp], ypv[c, wp]
                    diffs.append((mp - mm, pp - pm, pm - mm, pp - mp))
                for c in range(2):
                    up, down = src[c, l, w], src[c, l + 2, w]
                    total, nx, ny = four_n(faces, own[c], diffs[1 - c], c == 0)
                    total = total + e * (nx + ny + 8.0 * (up + down)) + 8.0 * (eu * up + ed * down)
                    inv = (gu, gv)[c][l, w]
                    store(c, l, r, (1.0 - omega) * src[c, l + 1, w] + omega * (inv * total))
            return carry

        lax.fori_loop(0, LAYERS, one, 0)

    def store_to(dst):
        def store(c, l, r, x):
            dst[c, l + 1, pl.ds(r, 8)] = x

        return store

    def store_out(c, l, r, x):
        out_ref[c, l, pl.ds(r - BASE, 8)] = x

    main_sweep(fa, s0, omegas[0], starts, store_to(fb))
    strip_sweep(s0, s1, omegas[0])
    main_sweep(fb, s1, omegas[1], starts, store_to(fa))
    strip_sweep(s1, s2, omegas[1])

    group = lane // CAP
    sub8 = lax.broadcasted_iota(jnp.int32, (8, 128), 0)
    sub64 = lax.broadcasted_iota(jnp.int32, (TX, 256), 0).astype(F32) + 1.0
    surf[...] = jnp.zeros((TX, 2 * TY), F32)

    def scatter(j, carry):
        sx = lax.rem(me_x - j + GX, GX)
        here = pl.ds(sx * GY, GY)
        pltpu.make_async_copy(recvb.at[here], recvb.at[here], a_recv.at[j]).wait()
        pltpu.make_async_copy(rrecv.at[here], rrecv.at[here], r_recv.at[j]).wait()
        rows = rrecv[here].reshape(GY, 128)
        parts = [
            jnp.sum(jnp.where(sub8 == group, rows[8 * h : 8 * h + 8], 0.0), axis=0, keepdims=True) for h in range(2)
        ]
        hot = jnp.where(jnp.concatenate(parts, axis=1) == sub64, 1.0, 0.0).astype(BF16)
        surf[...] += jnp.dot(hot, recvb[here].reshape(GY * CAP, 2 * TY), preferred_element_type=F32)
        return carry

    lax.fori_loop(0, GX, scatter, 0)

    for b in range(8):
        w = pl.ds(BASE + 8 * b, 8)
        cu = (4.0 * omegas[0]) * (gu[0, w] * surf[pl.ds(8 * b, 8), pl.ds(0, 128)])
        cv = (4.0 * omegas[0]) * (gv[0, w] * surf[pl.ds(8 * b, 8), pl.ds(128, 128)])
        c1[0, w] = cu
        c1[1, w] = cv
        ec[1, w] = jnp.where(lane < 8, roll(cu, 4), roll(cv, 12))

    def span_c(dx):
        if dx == 0:
            return pl.ds(BASE, TX), pl.ds(BASE, TX)
        if dx < 0:
            return pl.ds(BASE, 8), pl.ds(BASE + TX, 8)
        return pl.ds(BASE + TX - 8, 8), pl.ds(BASE - 8, 8)

    edges = []
    for i, (dx, dy) in enumerate(SIDES):
        src, dst = span_c(dx)
        edges.append(
            pltpu.make_async_remote_copy(
                ec.at[1, src], ec.at[1 - dy, dst], c_send.at[i], c_recv.at[i],
                device_id=at(dx, dy), device_id_type=MESH,
            )
        )
    for up, dx in ((0, -1), (1, 1)):
        src, dst = span_c(dx)
        edges.append(
            pltpu.make_async_remote_copy(
                c1.at[:, src], c1.at[:, dst], c_send.at[8 + up], c_recv.at[8 + up],
                device_id=at(dx, 0), device_id_type=MESH,
            )
        )
    for c in edges:
        c.start()

    main_sweep(fa, s2, omegas[2], [BASE + 8 * b for b in range(8)], store_out)
    right = lane < 64

    def join(a, b):
        return jnp.where(right, a, roll(b, 64))

    for r in starts:
        for wr in (r,):
            w = pl.ds(wr, 8)
            te[1, w] = join(roll(se[0, 0, w], 120), roll(se[1, 0, w], 120))
            for c in range(2):
                a, b = sg[0, 2 + c, w], sg[1, 2 + c, w]
                tg[0, c, w] = join(a, b)
                tg[1, c, w] = join(roll(a, 120), roll(b, 120))
    for b in range(1, 11):
        w = pl.ds(8 * b, 8)
        te[0, w] = join(se[0, 0, w], se[1, 0, w])

    for c in edges:
        c.wait()

    for b in range(1, 11):
        w = pl.ds(8 * b, 8)
        has = has_up if b == 1 else (has_down if b == 10 else 1.0)
        own, lef, rig = ec[1, w] * has, ec[0, w] * (has * has_left), ec[2, w] * (has * has_right)
        r_, l_ = jnp.where(low4, own, rig), jnp.where(low4, lef, own)
        tc1[0, w] = join(r_, l_)
        tc1[1, w] = join(roll(r_, 120), roll(l_, 120))
    for w, has in ((pl.ds(BASE - 8, 8), has_up), (pl.ds(BASE + TX, 8), has_down)):
        for c in range(2):
            c1[c, w] = c1[c, w] * has

    w1, w2 = omegas[1], omegas[2]
    again1 = 1.0 - w1 + w1 / omegas[0]
    for r in starts:
        w, wm, wp = pl.ds(r, 8), pl.ds(r - 1, 8), pl.ds(r + 1, 8)
        e = te[0, w]
        faces = (te[0, wm], te[0, wp], roll(e, 1), roll(e, 127))
        own, diffs, mid = [], [], []
        for c in range(2):
            m, z, p = tc1[c, wm], tc1[c, w], tc1[c, wp]
            mid.append(z)
            own.append((m, p, roll(z, 1), roll(z, 127)))
            dx = p - m
            diffs.append((roll(m, 127) - roll(m, 1), roll(p, 127) - roll(p, 1), roll(dx, 1), roll(dx, 127)))
        for c in range(2):
            total, nx, ny = four_n(faces, own[c], diffs[1 - c], c == 0)
            tc2[0, c, w] = again1 * mid[c] + w1 * (tg[0, c, w] * (total + e * (nx + ny)))
            tc2[1, c, w] = (8.0 * w1) * (tg[1, c, w] * ((e + te[1, w]) * mid[c]))

    def shift_all(src, strip, slot):
        for b in range(1, 11):
            w = pl.ds(8 * b, 8)
            for c in range(2):
                t = strip(c, w)
                ym, yp = shifted(src(c, w), roll(t, 60), roll(t, 124))
                ycm[slot, c, w] = ym
                ycp[slot, c, w] = yp

    def around(src, slot, l, w, wm, wp):
        e = et[l + 1, w]
        faces = (et[l + 1, wm], et[l + 1, wp], eym[l, w], eyp[l, w])
        own, diffs = [], []
        for c in range(2):
            own.append((src(c, wm), src(c, wp), ycm[slot, c, w], ycp[slot, c, w]))
            mm, mp, pm, pp = ycm[slot, c, wm], ycp[slot, c, wm], ycm[slot, c, wp], ycp[slot, c, wp]
            diffs.append((mp - mm, pp - pm, pm - mm, pp - mp))
        sums = []
        for c in range(2):
            total, nx, ny = four_n(faces, own[c], diffs[1 - c], c == 0)
            sums.append(total + e * (nx + ny))
        return sums

    shift_all(lambda c, w: c1[c, w], lambda c, w: tc1[c, w], 0)
    for r in starts:
        w, wm, wp = pl.ds(r, 8), pl.ds(r - 1, 8), pl.ds(r + 1, 8)
        sums = around(lambda c, x: c1[c, x], 0, 0, w, wm, wp)
        pair = et[1, w] + et[2, w]
        for c in range(2):
            z = c1[c, w]
            c2[0, c, w] = again1 * z + w1 * ((gu, gv)[c][0, w] * sums[c])
            c2[1, c, w] = (8.0 * w1) * ((gu, gv)[c][1, w] * (pair * z))
    for l in range(2):
        shift_all(lambda c, w: c2[l, c, w], lambda c, w: tc2[l, c, w], l)
    for b in range(8):
        r = BASE + 8 * b
        w, wm, wp = pl.ds(r, 8), pl.ds(r - 1, 8), pl.ds(r + 1, 8)
        pair = 8.0 * (et[1, w] + et[2, w])
        next_pair = (8.0 * w2) * (et[2, w] + et[3, w])
        for l in range(2):
            sums = around(lambda c, x: c2[l, c, x], l, l, w, wm, wp)
            for c in range(2):
                total = sums[c] + pair * c2[1 - l, c, w]
                x = (1.0 - w2) * c2[l, c, w] + w2 * ((gu, gv)[c][l, w] * total)
                c3_ref[c, l, pl.ds(8 * b, 8)] = x + (w2 / omegas[0]) * c1[c, w] if l == 0 else x
        for c in range(2):
            c3_ref[c, 2, pl.ds(8 * b, 8)] = (gu, gv)[c][2, w] * (next_pair * c2[1, c, w])

    pltpu.make_async_copy(sendb.at[pl.ds(0, TILES - 1)], sendb.at[pl.ds(0, TILES - 1)], a_send).wait()
    pltpu.make_async_copy(rsend.at[pl.ds(0, TILES - 1)], rsend.at[pl.ds(0, TILES - 1)], r_send).wait()


def padded(*lead):
    return pltpu.VMEM((*lead, ROWS, TY), F32)


def on_device(adjoint_prev, viscosity, friction, basal_velocity, ice_mask, misfit, block_tile, block_row):
    ice = ice_mask.astype(F32)
    hbm = pl.BlockSpec(memory_space=pltpu.HBM)
    vmem = pl.BlockSpec(memory_space=pltpu.VMEM)
    dma = pltpu.SemaphoreType.DMA
    base, corr = pl.pallas_call(
        kernel,
        out_shape=(
            jax.ShapeDtypeStruct((2, LAYERS, TX, TY), F32),
            jax.ShapeDtypeStruct((2, 3, TX, TY), F32),
        ),
        in_specs=[hbm] * 7,
        out_specs=(vmem, vmem),
        scratch_shapes=[
            padded(2, LAYERS + 2), padded(2, LAYERS + 2), padded(LAYERS + 2),
            padded(LAYERS), padded(LAYERS), padded(LAYERS), padded(LAYERS),
            padded(), padded(),
            pltpu.VMEM((4, 80, 128), F32), pltpu.VMEM((4, 80, 128), F32), pltpu.VMEM((4, 80, 128), F32),
            pltpu.VMEM((2, 62, 4, 128), F32), pltpu.VMEM((2, 62, 4, 128), F32),
            padded(2, 2, 2), padded(2, 2, 2), padded(2, 2, 2), padded(2, 2), padded(2, 6),
            padded(2), padded(2),
            pltpu.VMEM((1, SB), jnp.int32), pltpu.VMEM((1, SB), jnp.int32), pltpu.VMEM((1, SB), F32),
            pltpu.VMEM((2 * SB, TY), BF16), pltpu.VMEM((2 * SB, TY), F32), pltpu.VMEM((SB, 2 * TY), BF16),
            pltpu.VMEM((TILES, CAP, 2 * TY), BF16), pltpu.VMEM((TILES, CAP, 2 * TY), BF16),
            pltpu.VMEM((TILES, 1, 128), F32), pltpu.VMEM((TILES, 1, 128), F32),
            pltpu.VMEM((TX, 2 * TY), F32),
            padded(2), padded(2, 2), padded(3), padded(2), padded(2, 2),
            padded(2), padded(2, 2), padded(2, 2), padded(2, 2),
            dma((7,)), dma, dma((GX,)), dma, dma((GX,)),
            dma((8,)), dma((8,)), dma((2,)), dma((2,)), dma((10,)), dma((10,)),
            pltpu.SemaphoreType.REGULAR,
        ],
        compiler_params=pltpu.CompilerParams(
            collective_id=0, has_side_effects=True, vmem_limit_bytes=48 * 2**20
        ),
    )(
        adjoint_prev, viscosity, friction, ice,
        misfit.reshape(2 * SB, TY), block_tile.reshape(1, SB), block_row.reshape(1, SB),
    )
    adjoint = base + jnp.pad(corr, ((0, 0), (0, LAYERS - 3), (0, 0), (0, 0)))
    gradient = -friction * ice * (basal_velocity[0] * base[0, LAYERS - 1] + basal_velocity[1] * base[1, LAYERS - 1])
    return adjoint, gradient


def solution(mesh):
    placed = (
        P(None, None, "gx", "gy"),
        P(None, "gx", "gy"),
        P("gx", "gy"),
        P(None, "gx", "gy"),
        P("gx", "gy"),
        P(("gx", "gy"), None, None),
        P(("gx", "gy"), None),
        P(("gx", "gy")),
    )
    return jax.shard_map(
        on_device,
        mesh=mesh,
        in_specs=placed,
        out_specs=(P(None, None, "gx", "gy"), P("gx", "gy")),
        check_vma=False,
    )
```

time: 184 us -> 64.5 us (0.35)
  the two profiles are of different devices: /device:TPU:31 before, /device:TPU:1 now
where the time goes in v1:
time: 64.5 us; the launch traced here: 64 us
  Pallas kernels  55.2 us (86%)
  local copies, waits for them, and re-layouts  5.59 us (9%)
  other arithmetic  2.55 us (4%)
  between operations  0.66 us (1%)
    pallas_call x1, Pallas kernels, on_device(): pl.pallas_call(kernel, out_shape=(jax.ShapeDtypeStruct((2, LAYERS, TX, TY...  55.2 us
    unnamed x16, local copies, waits for them, and re-layouts  5.59 us

profile of v1, /device:TPU:1, one launch (start us, length us, event | category | flops | bytes accessed | tf_op | source)
XLA Modules:
  0.0 64.0 jit_solution(4596070112655690316)
XLA Ops:
  0.6 0.8 %convert_element_type.5.ice_hbm = f32[64,128]{1,0:T(8,128)S(1)} convert(s32[64,128]{1,0:T(8,128)} %param.12) | non-fusion elementwise | flops 8192 | bytes 65536 | tf_op jit(solution)/shard_map/convert_element_type | solution.py:580
  1.4 0.0 copy-start
  1.4 1.3 %copy-done = f32[2,20,64,128]{3,2,1,0:T(8,128)S(1)} copy-done((f32[2,20,64,128]{3,2,1,0:T(8,128)S(1)}, f32[2,20,64,128]{3,2,1,0:T(8,128)}, u32[]{:S(2)}) %copy-start) | copy-done | bytes 1310744
  2.7 0.0 copy-start.1
  2.7 1.1 %copy-done.1 = f32[20,64,128]{2,1,0:T(8,128)S(1)} copy-done((f32[20,64,128]{2,1,0:T(8,128)S(1)}, f32[20,64,128]{2,1,0:T(8,128)}, u32[]{:S(2)}) %copy-start.1) | copy-done | bytes 655384
  3.8 0.0 copy-start.2
  3.8 1.0 %copy-done.2 = bf16[1024,2,128]{2,1,0:T(2,128)(2,1)S(1)} copy-done((bf16[1024,2,128]{2,1,0:T(2,128)(2,1)S(1)}, bf16[1024,2,128]{2,1,0:T(2,128)(2,1)}, u32[]{:S(2)}) %copy-start.2) | copy-done | bytes 524312
  4.8 0.0 copy-start.3
  4.8 0.8 %copy-done.3 = f32[64,128]{1,0:T(8,128)S(1)} copy-done((f32[64,128]{1,0:T(8,128)S(1)}, f32[64,128]{1,0:T(8,128)}, u32[]{:S(2)}) %copy-start.3) | copy-done | bytes 32792
  5.6 0.0 copy-start.4
  5.6 0.7 %copy-done.4 = s32[1024,1]{0,1:T(1,128)S(1)} copy-done((s32[1024,1]{0,1:T(1,128)S(1)}, s32[1024,1]{0,1:T(1,128)}, u32[]{:S(2)}) %copy-start.4) | copy-done | bytes 4120
  6.3 0.0 copy-start.5
  6.3 0.7 %copy-done.5 = s32[1024]{0:T(1024)S(1)} copy-done((s32[1024]{0:T(1024)S(1)}, s32[1024]{0:T(1024)}, u32[]{:S(2)}) %copy-start.5) | copy-done | bytes 4120
  7.0 55.2 %shard_map.95 = (f32[2,20,64,128]{3,2,1,0:T(8,128)S(1)}, f32[2,3,64,128]{3,2,1,0:T(8,128)S(1)}) custom-call(f32[2,20,64,128]{3,2,1,0:T(8,128)S(1)} %copy-done, f32[20,64,128]{2,1,0:T(8,128)S(1)} %copy-done.1, f32[64,128]{1,0:T(8,128)S(1)} %copy-done.3, f32[64,128]{1,0:T(8,128)S(1)} %convert_element_type.5.ice_hbm, bf16[2048,128]{1,0:T(8,128)(2,1)S(1)} %bitcast.17, ...), custom_call_target="tpu_custom_call" | custom-call | tf_op jit(solution)/shard_map/pallas_call | solution.py:584
  62.2 0.0 copy-start.6
  62.2 0.0 copy-start.7
  62.2 1.2 %pad_add_fusion = f32[2,20,64,128]{3,2,1,0:T(8,128)} fusion(f32[2,20,64,128]{3,2,1,0:T(8,128)S(1)} %get-tuple-element.4, f32[2,3,64,128]{3,2,1,0:T(8,128)S(1)} %get-tuple-element.5), kind=kLoop, calls=%fused_computation | loop fusion | flops 327680 | bytes 2818048 | tf_op jit(solution)/shard_map/add | solution.py:618
  63.4 0.0 copy-done.6
  63.4 0.0 copy-done.7
  63.4 0.6 fusion.1
Async XLA Ops:
  1.4 1.3 %copy-start = (f32[2,20,64,128]{3,2,1,0:T(8,128)S(1)}, f32[2,20,64,128]{3,2,1,0:T(8,128)}, u32[]{:S(2)}) copy-start(f32[2,20,64,128]{3,2,1,0:T(8,128)} %adj_hbm.1) | copy-start | bytes 3932164
  2.7 1.1 %copy-start.1 = (f32[20,64,128]{2,1,0:T(8,128)S(1)}, f32[20,64,128]{2,1,0:T(8,128)}, u32[]{:S(2)}) copy-start(f32[20,64,128]{2,1,0:T(8,128)} %eta_hbm.1) | copy-start | bytes 1966084
  3.8 1.0 %copy-start.2 = (bf16[1024,2,128]{2,1,0:T(2,128)(2,1)S(1)}, bf16[1024,2,128]{2,1,0:T(2,128)(2,1)}, u32[]{:S(2)}) copy-start(bf16[1024,2,128]{2,1,0:T(2,128)(2,1)} %param.13) | copy-start | bytes 1572868
  4.8 0.8 %copy-start.3 = (f32[64,128]{1,0:T(8,128)S(1)}, f32[64,128]{1,0:T(8,128)}, u32[]{:S(2)}) copy-start(f32[64,128]{1,0:T(8,128)} %fric_hbm.1) | copy-start | bytes 98308
  5.6 0.7 %copy-start.4 = (s32[1024,1]{0,1:T(1,128)S(1)}, s32[1024,1]{0,1:T(1,128)}, u32[]{:S(2)}) copy-start(s32[1024,1]{0,1:T(1,128)} %param.14) | copy-start | bytes 12292
  6.3 0.7 %copy-start.5 = (s32[1024]{0:T(1024)S(1)}, s32[1024]{0:T(1024)}, u32[]{:S(2)}) copy-start(s32[1024]{0:T(1024)} %param.15) | copy-start | bytes 12292
  62.2 1.2 %copy-start.6 = (s32[64,128]{1,0:T(8,128)S(1)}, s32[64,128]{1,0:T(8,128)}, u32[]{:S(2)}) copy-start(s32[64,128]{1,0:T(8,128)} %param.12) | copy-start | bytes 98308
  62.2 1.2 %copy-start.7 = (f32[2,64,128]{2,1,0:T(8,128)S(1)}, f32[2,64,128]{2,1,0:T(8,128)}, u32[]{:S(2)}) copy-start(f32[2,64,128]{2,1,0:T(8,128)} %param.11) | copy-start | bytes 196612

commit v2 on v1

v2 whole, which is shorter than its diff:
```python
import functools
import math

import jax
import jax.numpy as jnp
from jax import lax
from jax.experimental import pallas as pl
from jax.experimental.pallas import tpu as pltpu
from jax.sharding import PartitionSpec as P

ITERS = 3
GX = 8
GY = 16
TILES = GX * GY
CAP = 16
SB = 1024
LAYERS = 20
TX = 64
TY = 128
BASE = 16
ROWS = 96
F32 = jnp.float32
BF16 = jnp.bfloat16
MESH = pl.DeviceIdType.MESH
SIDES = ((0, -1), (0, 1), (-1, 0), (1, 0), (-1, -1), (-1, 1), (1, -1), (1, 1))


def omega_list(count):
    return [1.0 / (1.3 + 1.2 * math.cos((2 * k + 1) * math.pi / (2 * count))) for k in range(count)]


def lanes():
    return lax.broadcasted_iota(jnp.int32, (8, 128), 1)


def roll(x, shift):
    return pltpu.roll(x, shift, 1)


def four_n(e, f, o, heavy_x):
    exm, exp_, eym, eyp = e
    fxm, fxp, fym, fyp = f
    dym, dyp, dxm, dxp = o
    if heavy_x:
        x = exm * (4.0 * fxm - dym) + exp_ * (4.0 * fxp + dyp)
        y = eym * (2.0 * fym - dxm) + eyp * (2.0 * fyp + dxp)
        return 2.0 * x + y, 8.0 * (fxm + fxp), 2.0 * (fym + fyp)
    x = exm * (2.0 * fxm - dym) + exp_ * (2.0 * fxp + dyp)
    y = eym * (4.0 * fym - dxm) + eyp * (4.0 * fyp + dxp)
    return x + 2.0 * y, 2.0 * (fxm + fxp), 8.0 * (fym + fyp)


def kernel(
    adj_hbm, eta_hbm, fric_hbm, vel_hbm, ice_hbm, mis_hbm, tile_hbm, row_hbm,
    out_hbm, grad_hbm,
    fa, fb, et, eym, eyp, gu, gv, icei, icef, frip,
    e_own, e_left, e_right, pr, rr, s0, s1, s2, se, si, sf, sg, sn, sym, syp, h0, h1, h2, he, yma, ypa, ymb, ypb,
    vel_v, grad_v, tile_v, row_v, slot_v, mis_v, mis_f, vals, sendb, recvb, rsend, rrecv, surf,
    c1, c2, c3, ec, tc1, tc2, tym, typ, te, tg, ycm, ycp,
    in_sem, a_send, a_recv, r_send, r_recv, h_send, h_recv, q_send, q_recv, c_send, c_recv, o_sem, bar2,
):
    me_x = lax.axis_index("gx")
    me_y = lax.axis_index("gy")
    me = me_x * GY + me_y
    omegas = omega_list(ITERS)

    def at(dx, dy):
        return (lax.rem(me_x + dx + GX, GX), lax.rem(me_y + dy + GY, GY))

    ins = [
        (tile_hbm, tile_v), (row_hbm, row_v), (mis_hbm, mis_v),
        (vel_hbm, vel_v), (ice_hbm, icei), (fric_hbm, frip.at[pl.ds(BASE, TX)]),
        (eta_hbm, et.at[pl.ds(1, LAYERS), pl.ds(BASE, TX)]),
        (adj_hbm, fa.at[:, pl.ds(1, LAYERS), pl.ds(BASE, TX)]),
    ]
    loads = [pltpu.make_async_copy(s, d, in_sem.at[i]) for i, (s, d) in enumerate(ins)]
    for c in loads:
        c.start()
    barrier = pltpu.get_barrier_semaphore()
    for k in range(1, GY):
        pl.semaphore_signal(barrier, inc=1, device_id=at(0, k), device_id_type=MESH)
    for k in range(1, GX):
        pl.semaphore_signal(barrier, inc=1, device_id=at(k, 0), device_id_type=MESH)
    for dx, dy in SIDES[4:]:
        pl.semaphore_signal(barrier, inc=1, device_id=at(dx, dy), device_id_type=MESH)


    for c in loads[4:]:
        c.wait()
    lane = lanes()

    def build(rb, carry):
        r = pl.multiple_of(BASE + rb * 8, 8)
        q = pl.multiple_of(8 + rb * 8, 8)
        ice = icei[pl.ds(pl.multiple_of(rb * 8, 8), 8)].astype(F32)
        icef[pl.ds(r, 8)] = ice
        edge = jnp.zeros((8, 128), F32)

        def put(acc, x, unit):
            return jnp.where((lane >= 8 * unit) & (lane < 8 * unit + 8), roll(x, (8 * unit + 4) % 128), acc)

        for kind in range(3):
            acc = jnp.zeros((8, 128), F32)
            for l in range(LAYERS):
                if kind < 2:
                    x = ice * fa[kind, l + 1, pl.ds(r, 8)]
                    fa[kind, l + 1, pl.ds(r, 8)] = x
                else:
                    x = et[l + 1, pl.ds(r, 8)]
                if l < 16:
                    acc = put(acc, x, l)
                else:
                    edge = put(edge, x, 4 * kind + l - 16)
            e_own[kind, pl.ds(q, 8)] = acc
        edge = put(edge, ice, 12)
        edge = put(edge, frip[pl.ds(r, 8)], 13)
        e_own[3, pl.ds(q, 8)] = edge
        return carry

    lax.fori_loop(0, 8, build, 0)

    def pack_rows(l, carry):
        for up in range(2):
            r = BASE + (TX - 4) * up
            pr[up, l] = fa[0, l + 1, pl.ds(r, 4)]
            pr[up, LAYERS + l] = fa[1, l + 1, pl.ds(r, 4)]
            pr[up, 2 * LAYERS + l] = et[l + 1, pl.ds(r, 4)]
        return carry

    lax.fori_loop(0, LAYERS, pack_rows, 0)
    for up in range(2):
        r = BASE + (TX - 4) * up
        pr[up, 3 * LAYERS] = icef[pl.ds(r, 4)]
        pr[up, 3 * LAYERS + 1] = frip[pl.ds(r, 4)]

    pl.semaphore_wait(barrier, GX + GY + 2)
    for k in range(1, GX):
        pl.semaphore_signal(bar2, inc=1, device_id=at(k, 0), device_id_type=MESH)

    def span(dx):
        if dx == 0:
            return pl.ds(8, TX), pl.ds(8, TX)
        return (pl.ds(8, 8), pl.ds(72, 8)) if dx < 0 else (pl.ds(64, 8), pl.ds(0, 8))

    halos = []
    for i, (dx, dy) in enumerate(SIDES):
        src, dst = span(dx)
        land = (e_right, e_own, e_left)[dy + 1]
        halos.append(
            pltpu.make_async_remote_copy(
                e_own.at[:, src], land.at[:, dst], h_send.at[i], h_recv.at[i],
                device_id=at(dx, dy), device_id_type=MESH,
            )
        )
    for up, dx in ((0, -1), (1, 1)):
        halos.append(
            pltpu.make_async_remote_copy(
                pr.at[up], rr.at[1 - up], q_send.at[up], q_recv.at[up], device_id=at(dx, 0), device_id_type=MESH
            )
        )
    for c in halos:
        c.start()

    loads[0].wait()
    loads[1].wait()
    ii = lax.broadcasted_iota(jnp.int32, (256, 512), 0)
    jj = lax.broadcasted_iota(jnp.int32, (256, 512), 1)
    tri = jnp.where((ii < jj) | (jj >= 256), 1.0, 0.0).astype(BF16)
    tsub = lax.broadcasted_iota(jnp.int32, (TILES, 256), 0)
    running = jnp.zeros((TILES, 256), F32)
    rmat = jnp.zeros((TILES, 128), F32)
    for c in range(4):
        t = tile_v[:, pl.ds(256 * c, 256)]
        hit = jnp.where(t == tsub, 1.0, 0.0)
        hot = hit.astype(BF16)
        sums = jnp.dot(hot, tri, preferred_element_type=F32)
        pos = jnp.sum(hit * (running + sums[:, :256]), axis=0, keepdims=True)
        running = running + sums[:, 256:]
        slot_v[:, pl.ds(256 * c, 256)] = t.astype(F32) * float(CAP) + pos
        z = jnp.where(
            pos == (tsub & (CAP - 1)).astype(F32), row_v[:, pl.ds(256 * c, 256)].astype(F32) + 1.0, 0.0
        ).astype(BF16)
        rmat = rmat + lax.dot_general(hot, z, (((1,), (1,)), ((), ())), preferred_element_type=F32)
    rsend[...] = rmat.reshape(TILES, 1, 128)

    loads[2].wait()

    def widen(i, carry):
        mis_f[pl.ds(pl.multiple_of(i * 128, 128), 128)] = mis_v[pl.ds(pl.multiple_of(i * 128, 128), 128)].astype(F32)
        return carry

    lax.fori_loop(0, 16, widen, 0)
    for c in range(2):
        for i in range(8):
            vals[pl.ds(128 * i, 128), pl.ds(128 * c, 128)] = mis_f[pl.ds(256 * i + c, 128, stride=2)].astype(BF16)

    def pack(px, carry):
        want = (px * (GY * CAP)).astype(F32) + lax.broadcasted_iota(jnp.int32, (256, SB), 0).astype(F32)
        sel = jnp.where(slot_v[...] == want, 1.0, 0.0).astype(BF16)
        got = jnp.dot(sel, vals[...], preferred_element_type=F32).astype(BF16)
        sendb[pl.ds(px * GY, GY)] = got.reshape(GY, CAP, 2 * TY)
        return carry

    lax.fori_loop(0, GX, pack, 0)

    pl.semaphore_wait(bar2, GX - 1)
    own_values = pltpu.make_async_copy(sendb.at[me], recvb.at[me], a_recv.at[0])
    own_rows = pltpu.make_async_copy(rsend.at[me], rrecv.at[me], r_recv.at[0])
    own_values.start()
    own_rows.start()

    def send(j, carry):
        px = lax.rem(me_x + j, GX)

        def one(k, inner):
            py = lax.rem(me_y + k, GY)
            d = px * GY + py
            pltpu.make_async_remote_copy(
                sendb.at[d], recvb.at[me], a_send, a_recv.at[j], device_id=(px, py), device_id_type=MESH
            ).start()
            pltpu.make_async_remote_copy(
                rsend.at[d], rrecv.at[me], r_send, r_recv.at[j], device_id=(px, py), device_id_type=MESH
            ).start()
            return inner

        lax.fori_loop(jnp.where(j == 0, 1, 0), GY, one, 0)
        return carry

    lax.fori_loop(0, GX, send, 0)

    zero = jnp.zeros((8, 128), F32)

    def clear(r, carry):
        q = pl.ds(pl.multiple_of(r * 8, 8), 8)
        for end in (0, LAYERS + 1):
            et[end, q] = zero
            for c in range(2):
                fa[c, end, q] = zero
                fb[c, end, q] = zero
        return carry

    lax.fori_loop(0, ROWS // 8, clear, 0)

    def flag(cond):
        return jnp.where(cond, 1.0, 0.0).astype(F32)

    has_up, has_down = flag(me_x > 0), flag(me_x < GX - 1)
    has_left, has_right = flag(me_y > 0), flag(me_y < GY - 1)
    for c in halos:
        c.wait()

    def unpack_rows(l, carry):
        for side, r, has in ((0, BASE - 4, has_up), (1, BASE + TX, has_down)):
            fa[0, l + 1, pl.ds(r, 4)] = rr[side, l] * has
            fa[1, l + 1, pl.ds(r, 4)] = rr[side, LAYERS + l] * has
            et[l + 1, pl.ds(r, 4)] = rr[side, 2 * LAYERS + l] * has
        return carry

    lax.fori_loop(0, LAYERS, unpack_rows, 0)
    for side, r, has in ((0, BASE - 4, has_up), (1, BASE + TX, has_down)):
        icef[pl.ds(r, 4)] = rr[side, 3 * LAYERS] * has
        frip[pl.ds(r, 4)] = rr[side, 3 * LAYERS + 1] * has

    low4 = (lane & 7) < 4

    def tile_units(x):
        x = jnp.where(lane < 8, x, 0.0)
        for s in (8, 16, 32, 64):
            x = x + roll(x, s)
        return x

    right = lane < 64
    half = (lane & 63) < 32

    def join(a, b):
        return jnp.where(right, a, roll(b, 64))

    def halo(dst, x, w):
        dst[0, w] = jnp.where(low4, x[1], x[0])
        dst[1, w] = jnp.where(low4, roll(x[2], 64), x[2])

    for b in range(10):
        q = pl.ds(8 * b, 8)
        w = pl.ds(8 + 8 * b, 8)
        has = has_up if b == 0 else (has_down if b == 9 else 1.0)
        r_, l_ = [], []
        for kind in range(4):
            own = e_own[kind, q] * has
            r_.append(jnp.where(low4, own, e_right[kind, q] * (has * has_right)))
            l_.append(jnp.where(low4, e_left[kind, q] * (has * has_left), own))
        for c in range(3):
            turn = (0, 96, 64)[c]
            mr, ml = (roll(r_[3], turn), roll(l_[3], turn)) if turn else (r_[3], l_[3])
            x = (r_[c], l_[c], jnp.where(half, join(mr, ml), 0.0))
            for p in range(3):
                if c < 2:
                    s0[c, p, w] = x[p]
                else:
                    se[p, w] = x[p]
            halo((h0.at[0], h0.at[1], he)[c], x, w)
        a, d = tile_units(roll(r_[3], 32)), tile_units(roll(l_[3], 32))
        si[0, w] = a
        si[1, w] = d
        si[2, w] = jnp.where(half, jnp.where(right, a, d), 0.0)
        sf[w] = jnp.where(half & ((lane & 63) >= 24), join(roll(r_[3], 48), roll(l_[3], 48)), 0.0)

    def inverse(dx4, dy4, rest, ice):
        du = 4.0 * dx4 + dy4 + rest
        dv = dx4 + 4.0 * dy4 + rest
        live = ice > 0.0
        r = jnp.where(live, 0.25, 0.0) / jnp.where(live, du * dv, 1.0)
        return r * dv, r * du

    def neighbours(x, p):
        if p < 2:
            return (
                jnp.where(lane < 8, 0.0, roll(x[p], 8)),
                jnp.where(lane < 120, roll(x[p], 120), roll(x[2], 120 if p == 0 else 56)),
            )
        up = jnp.where(right, jnp.where(lane < 8, roll(x[0], 8), roll(x[2], 8)), 0.0)
        return (
            jnp.where(right, up, jnp.where(lane < 72, roll(x[1], 72), roll(x[2], 8))),
            roll(x[2], 120),
        )

    starts = [14 + 8 * b for b in range(9)]

    for r in starts:
        w = pl.ds(r, 8)
        es = [se[p, w] for p in range(3)]
        for p, e in enumerate(es):
            up, down = neighbours(es, p)
            count = jnp.where((lane < 8) if p < 2 else ((lane & 63) >= 24), 1.0, 2.0)
            dx4 = 0.5 * (se[p, pl.ds(r - 1, 8)] + se[p, pl.ds(r + 1, 8)]) + e
            ym, yp = roll(e, 1), roll(e, 127)
            for k, x in enumerate((ym, yp, up, down)):
                sn[k, p, w] = x
            dy4 = 0.5 * (ym + yp) + e
            rest = 2.0 * (up + down + count * e)
            if p == 2:
                rest = rest + sf[w]
            a, b = inverse(dx4, dy4, rest, si[p, w])
            sg[0, p, w] = a
            sg[1, p, w] = b

    def shifted(x, beyond):
        return roll(jnp.where(lane == 127, beyond, x), 1), roll(jnp.where(lane == 0, beyond, x), 127)

    def main_inverse(l):
        g = l // 16
        unit = l - 16 * g
        turn = 124 - 8 * unit
        bottom = flag(l == LAYERS - 1)
        count = 2.0 - flag(l == 0) - bottom
        for r in starts:
            w = pl.ds(r, 8)
            e = et[l + 1, w]
            ym, yp = shifted(e, roll(he[g, w], turn))
            eym[l, w] = ym
            eyp[l, w] = yp
            dx4 = 0.5 * (et[l + 1, pl.ds(r - 1, 8)] + et[l + 1, pl.ds(r + 1, 8)]) + e
            dy4 = 0.5 * (ym + yp) + e
            rest = 2.0 * (et[l, w] + et[l + 2, w] + count * e) + bottom * frip[w]
            a, b = inverse(dx4, dy4, rest, icef[w])
            gu[l, w] = a
            gv[l, w] = b

    def inverses(i, carry):
        for k in range(4):
            main_inverse(4 * i + k)
        return carry

    lax.fori_loop(0, LAYERS // 4, inverses, 0)

    def strip_sweep(src, dst, beyond, omega):
        for b in range(1, 11):
            w = pl.ds(8 * b, 8)
            for c in range(2):
                for p in range(3):
                    x = src[c, p, w]
                    sym[c, p, w] = roll(x, 1)
                    syp[c, p, w] = roll(x, 127)
        for r in starts:
            w, wm, wp = pl.ds(r, 8), pl.ds(r - 1, 8), pl.ds(r + 1, 8)
            mid = [[src[c, p, w] for p in range(3)] for c in range(2)]
            new = [[None] * 3 for _ in range(2)]
            for p in range(3):
                e, eu, ed = se[p, w], sn[2, p, w], sn[3, p, w]
                faces = (se[p, wm], se[p, wp], sn[0, p, w], sn[1, p, w])
                own, diffs = [], []
                for c in range(2):
                    own.append((src[c, p, wm], src[c, p, wp], sym[c, p, w], syp[c, p, w]))
                    mm, mp, pm, pp = sym[c, p, wm], syp[c, p, wm], sym[c, p, wp], syp[c, p, wp]
                    diffs.append((mp - mm, pp - pm, pm - mm, pp - mp))
                for c in range(2):
                    up, down = neighbours(mid[c], p)
                    total, nx, ny = four_n(faces, own[c], diffs[1 - c], c == 0)
                    total = total + e * (nx + ny + 8.0 * (up + down)) + 8.0 * (eu * up + ed * down)
                    new[c][p] = (1.0 - omega) * mid[c][p] + omega * (sg[c, p, w] * total)
                    dst[c, p, w] = new[c][p]
            for c in range(2):
                halo(beyond.at[c], new[c], w)

    def main_sweep(src, beyond, omega, first, rows_at, store):
        def shift(l, ym_, yp_):
            g = l // 16
            turn = 124 - 8 * (l - 16 * g)
            for b in range(9):
                w = pl.ds(first + 8 * b, 8)
                for c in range(2):
                    ym, yp = shifted(src[c, l + 1, w], roll(beyond[c, g, w], turn))
                    ym_[c, w] = ym
                    yp_[c, w] = yp

        def sweep(l, ym_, yp_):
            for r in rows_at:
                w, wm, wp = pl.ds(r, 8), pl.ds(r - 1, 8), pl.ds(r + 1, 8)
                e, eu, ed = et[l + 1, w], et[l, w], et[l + 2, w]
                faces = (et[l + 1, wm], et[l + 1, wp], eym[l, w], eyp[l, w])
                own, diffs = [], []
                for c in range(2):
                    own.append((src[c, l + 1, wm], src[c, l + 1, wp], ym_[c, w], yp_[c, w]))
                    mm, mp, pm, pp = ym_[c, wm], yp_[c, wm], ym_[c, wp], yp_[c, wp]
                    diffs.append((mp - mm, pp - pm, pm - mm, pp - mp))
                for c in range(2):
                    up, down = src[c, l, w], src[c, l + 2, w]
                    total, nx, ny = four_n(faces, own[c], diffs[1 - c], c == 0)
                    total = total + e * (nx + ny + 8.0 * (up + down)) + 8.0 * (eu * up + ed * down)
                    inv = (gu, gv)[c][l, w]
                    store(c, l, r, (1.0 - omega) * src[c, l + 1, w] + omega * (inv * total))

        def pair(i, carry):
            l = 2 * i
            shift(l + 1, ymb, ypb)
            sweep(l, yma, ypa)
            shift(l + 2, yma, ypa)
            sweep(l + 1, ymb, ypb)
            return carry

        shift(0, yma, ypa)
        lax.fori_loop(0, LAYERS // 2, pair, 0)

    def store_to(dst):
        def store(c, l, r, x):
            dst[c, l + 1, pl.ds(r, 8)] = x

        return store

    main_sweep(fa, h0, omegas[0], 13, starts, store_to(fb))
    strip_sweep(s0, s1, h1, omegas[0])
    main_sweep(fb, h1, omegas[1], 14, [15 + 8 * b for b in range(9)], store_to(fa))

    group = lane // CAP
    sub8 = lax.broadcasted_iota(jnp.int32, (8, 128), 0)
    sub64 = lax.broadcasted_iota(jnp.int32, (TX, 256), 0).astype(F32) + 1.0
    for j in range(GX):
        here = pl.ds(lax.rem(me_x - j + GX, GX) * GY, GY)
        pltpu.make_async_copy(recvb.at[here], recvb.at[here], a_recv.at[j]).wait()
        pltpu.make_async_copy(rrecv.at[here], rrecv.at[here], r_recv.at[j]).wait()
    total = jnp.zeros((TX, 2 * TY), F32)
    for j in range(GX):
        rows = rrecv[pl.ds(j * GY, GY)].reshape(GY, 128)
        parts = [
            jnp.sum(jnp.where(sub8 == group, rows[8 * h : 8 * h + 8], 0.0), axis=0, keepdims=True) for h in range(2)
        ]
        hot = jnp.where(jnp.concatenate(parts, axis=1) == sub64, 1.0, 0.0).astype(BF16)
        got = recvb[pl.ds(j * GY, GY)].reshape(GY * CAP, 2 * TY)
        total = total + jnp.dot(hot, got, preferred_element_type=F32)
    surf[...] = total

    for b in range(8):
        w = pl.ds(BASE + 8 * b, 8)
        cu = (4.0 * omegas[0]) * (gu[0, w] * surf[pl.ds(8 * b, 8), pl.ds(0, 128)])
        cv = (4.0 * omegas[0]) * (gv[0, w] * surf[pl.ds(8 * b, 8), pl.ds(128, 128)])
        c1[0, w] = cu
        c1[1, w] = cv
        ec[1, w] = jnp.where(lane < 8, roll(cu, 4), roll(cv, 12))

    def span_c(dx):
        if dx == 0:
            return pl.ds(BASE, TX), pl.ds(BASE, TX)
        if dx < 0:
            return pl.ds(BASE, 8), pl.ds(BASE + TX, 8)
        return pl.ds(BASE + TX - 8, 8), pl.ds(BASE - 8, 8)

    edges = []
    for i, (dx, dy) in enumerate(SIDES):
        src, dst = span_c(dx)
        edges.append(
            pltpu.make_async_remote_copy(
                ec.at[1, src], ec.at[1 - dy, dst], c_send.at[i], c_recv.at[i],
                device_id=at(dx, dy), device_id_type=MESH,
            )
        )
    for up, dx in ((0, -1), (1, 1)):
        src, dst = span_c(dx)
        edges.append(
            pltpu.make_async_remote_copy(
                c1.at[:, src], c1.at[:, dst], c_send.at[8 + up], c_recv.at[8 + up],
                device_id=at(dx, 0), device_id_type=MESH,
            )
        )
    for c in edges:
        c.start()

    strip_sweep(s1, s2, h2, omegas[1])
    main_sweep(fa, h2, omegas[2], 15, [BASE + 8 * b for b in range(8)], store_to(fb))
    kept = pl.ds(4, LAYERS - 3)
    out_low = pltpu.make_async_copy(fb.at[:, kept, pl.ds(BASE, TX)], out_hbm.at[:, pl.ds(3, LAYERS - 3)], o_sem.at[0])
    out_low.start()
    loads[3].wait()
    for b in range(8):
        r, w = pl.ds(8 * b, 8), pl.ds(BASE + 8 * b, 8)
        flow = vel_v[0, r] * fb[0, LAYERS, w] + vel_v[1, r] * fb[1, LAYERS, w]
        grad_v[r] = -frip[w] * icef[w] * flow
    out_grad = pltpu.make_async_copy(grad_v, grad_hbm, o_sem.at[2])
    out_grad.start()
    for r in starts:
        w = pl.ds(r, 8)
        te[1, w] = join(roll(se[0, w], 120), roll(se[1, w], 120))
        for c in range(2):
            a, b = sg[c, 0, w], sg[c, 1, w]
            tg[0, c, w] = join(a, b)
            tg[1, c, w] = join(roll(a, 120), roll(b, 120))
    for b in range(1, 11):
        w = pl.ds(8 * b, 8)
        e = join(se[0, w], se[1, w])
        te[0, w] = e
        te[2, w] = roll(e, 1)
        te[3, w] = roll(e, 127)

    for c in edges:
        c.wait()

    for w, has in ((pl.ds(BASE - 8, 8), has_up), (pl.ds(BASE + TX, 8), has_down)):
        for c in range(2):
            c1[c, w] = c1[c, w] * has
    for b in range(1, 11):
        w = pl.ds(8 * b, 8)
        has = has_up if b == 1 else (has_down if b == 10 else 1.0)
        own, lef, rig = ec[1, w] * has, ec[0, w] * (has * has_left), ec[2, w] * (has * has_right)
        r_, l_, out = jnp.where(low4, own, rig), jnp.where(low4, lef, own), jnp.where(low4, lef, rig)
        for c in range(2):
            ym, yp = shifted(c1[c, w], roll(out, 124 - 8 * c))
            ycm[0, c, w] = ym
            ycp[0, c, w] = yp
            t = jnp.where(right, roll(r_, 120), roll(l_, 56)) if c else join(r_, l_)
            tc1[c, w] = t
            tym[c, w] = roll(t, 1)
            typ[c, w] = roll(t, 127)

    w1, w2 = omegas[1], omegas[2]
    again1 = 1.0 - w1 + w1 / omegas[0]
    for r in starts:
        w, wm, wp = pl.ds(r, 8), pl.ds(r - 1, 8), pl.ds(r + 1, 8)
        e = te[0, w]
        faces = (te[0, wm], te[0, wp], te[2, w], te[3, w])
        own, diffs, mid = [], [], []
        for c in range(2):
            mid.append(tc1[c, w])
            own.append((tc1[c, wm], tc1[c, wp], tym[c, w], typ[c, w]))
            mm, mp, pm, pp = tym[c, wm], typ[c, wm], tym[c, wp], typ[c, wp]
            diffs.append((mp - mm, pp - pm, pm - mm, pp - mp))
        for c in range(2):
            total, nx, ny = four_n(faces, own[c], diffs[1 - c], c == 0)
            tc2[0, c, w] = again1 * mid[c] + w1 * (tg[0, c, w] * (total + e * (nx + ny)))
            tc2[1, c, w] = (8.0 * w1) * (tg[1, c, w] * ((e + te[1, w]) * mid[c]))

    def shift_all(src, strip, slot):
        for b in range(1, 11):
            w = pl.ds(8 * b, 8)
            for c in range(2):
                t = strip(c, w)
                ym, yp = shifted(src(c, w), jnp.where(right, roll(t, 124), roll(t, 60)))
                ycm[slot, c, w] = ym
                ycp[slot, c, w] = yp

    def around(src, slot, l, w, wm, wp):
        e = et[l + 1, w]
        faces = (et[l + 1, wm], et[l + 1, wp], eym[l, w], eyp[l, w])
        own, diffs = [], []
        for c in range(2):
            own.append((src(c, wm), src(c, wp), ycm[slot, c, w], ycp[slot, c, w]))
            mm, mp, pm, pp = ycm[slot, c, wm], ycp[slot, c, wm], ycm[slot, c, wp], ycp[slot, c, wp]
            diffs.append((mp - mm, pp - pm, pm - mm, pp - mp))
        sums = []
        for c in range(2):
            total, nx, ny = four_n(faces, own[c], diffs[1 - c], c == 0)
            sums.append(total + e * (nx + ny))
        return sums

    for r in starts:
        w, wm, wp = pl.ds(r, 8), pl.ds(r - 1, 8), pl.ds(r + 1, 8)
        sums = around(lambda c, x: c1[c, x], 0, 0, w, wm, wp)
        pair = et[1, w] + et[2, w]
        for c in range(2):
            z = c1[c, w]
            c2[0, c, w] = again1 * z + w1 * ((gu, gv)[c][0, w] * sums[c])
            c2[1, c, w] = (8.0 * w1) * ((gu, gv)[c][1, w] * (pair * z))
    for l in range(2):
        shift_all(lambda c, w: c2[l, c, w], lambda c, w: tc2[l, c, w], l)
    for b in range(8):
        r = BASE + 8 * b
        w, wm, wp = pl.ds(r, 8), pl.ds(r - 1, 8), pl.ds(r + 1, 8)
        pair = 8.0 * (et[1, w] + et[2, w])
        next_pair = (8.0 * w2) * (et[2, w] + et[3, w])
        for l in range(2):
            sums = around(lambda c, x: c2[l, c, x], l, l, w, wm, wp)
            for c in range(2):
                total = sums[c] + pair * c2[1 - l, c, w]
                x = (1.0 - w2) * c2[l, c, w] + w2 * ((gu, gv)[c][l, w] * total)
                if l == 0:
                    x = x + (w2 / omegas[0]) * c1[c, w]
                c3[c, l, pl.ds(8 * b, 8)] = fb[c, l + 1, w] + x
        for c in range(2):
            x = (gu, gv)[c][2, w] * (next_pair * c2[1, c, w])
            c3[c, 2, pl.ds(8 * b, 8)] = fb[c, 3, w] + x

    out_high = pltpu.make_async_copy(c3, out_hbm.at[:, pl.ds(0, 3)], o_sem.at[1])
    out_high.start()

    pltpu.make_async_copy(sendb.at[pl.ds(0, TILES - 1)], sendb.at[pl.ds(0, TILES - 1)], a_send).wait()
    pltpu.make_async_copy(rsend.at[pl.ds(0, TILES - 1)], rsend.at[pl.ds(0, TILES - 1)], r_send).wait()
    out_low.wait()
    out_high.wait()
    out_grad.wait()


def hand_on(adj_ref, grad_ref, out_ref, grad_out_ref, held, grad_held, in_sem, out_sem):
    pairs = []
    for c in range(2):
        for k in range(4):
            at = (c, pl.ds(k * (LAYERS // 4), LAYERS // 4))
            pairs.append((adj_ref.at[at], held.at[at], out_ref.at[at]))
    pairs.append((grad_ref, grad_held, grad_out_ref))
    first = [pltpu.make_async_copy(a, b, in_sem.at[i]) for i, (a, b, _) in enumerate(pairs)]
    second = [pltpu.make_async_copy(b, d, out_sem.at[i]) for i, (_, b, d) in enumerate(pairs)]
    for c in first:
        c.start()
    for c, d in zip(first, second):
        c.wait()
        d.start()
    for d in second:
        d.wait()


def padded(*lead):
    return pltpu.VMEM((*lead, ROWS, TY), F32)


def on_device(adjoint_prev, viscosity, friction, basal_velocity, ice_mask, misfit, block_tile, block_row):
    hbm = pl.BlockSpec(memory_space=pltpu.HBM)
    dma = pltpu.SemaphoreType.DMA
    shapes = (jax.ShapeDtypeStruct((2, LAYERS, TX, TY), F32), jax.ShapeDtypeStruct((TX, TY), F32))
    results = pl.pallas_call(
        kernel,
        out_shape=shapes,
        in_specs=[hbm] * 8,
        out_specs=(hbm, hbm),
        scratch_shapes=[
            padded(2, LAYERS + 2), padded(2, LAYERS + 2), padded(LAYERS + 2),
            padded(LAYERS), padded(LAYERS), padded(LAYERS), padded(LAYERS),
            pltpu.VMEM((TX, TY), jnp.int32), padded(), padded(),
            pltpu.VMEM((4, 80, 128), F32), pltpu.VMEM((4, 80, 128), F32), pltpu.VMEM((4, 80, 128), F32),
            pltpu.VMEM((2, 62, 4, 128), F32), pltpu.VMEM((2, 62, 4, 128), F32),
            padded(2, 3), padded(2, 3), padded(2, 3), padded(3), padded(3), padded(), padded(2, 3),
            padded(4, 3), padded(2, 3), padded(2, 3),
            padded(2, 2), padded(2, 2), padded(2, 2), padded(2),
            padded(2), padded(2), padded(2), padded(2),
            pltpu.VMEM((2, TX, TY), F32), pltpu.VMEM((TX, TY), F32),
            pltpu.VMEM((1, SB), jnp.int32), pltpu.VMEM((1, SB), jnp.int32), pltpu.VMEM((1, SB), F32),
            pltpu.VMEM((2 * SB, TY), BF16), pltpu.VMEM((2 * SB, TY), F32), pltpu.VMEM((SB, 2 * TY), BF16),
            pltpu.VMEM((TILES, CAP, 2 * TY), BF16), pltpu.VMEM((TILES, CAP, 2 * TY), BF16),
            pltpu.VMEM((TILES, 1, 128), F32), pltpu.VMEM((TILES, 1, 128), F32),
            pltpu.VMEM((TX, 2 * TY), F32),
            padded(2), padded(2, 2), pltpu.VMEM((2, 3, TX, TY), F32),
            padded(3), padded(2), padded(2, 2), padded(2), padded(2),
            padded(4), padded(2, 2), padded(2, 2), padded(2, 2),
            dma((8,)), dma, dma((GX,)), dma, dma((GX,)),
            dma((8,)), dma((8,)), dma((2,)), dma((2,)), dma((10,)), dma((10,)), dma((3,)),
            pltpu.SemaphoreType.REGULAR,
        ],
        compiler_params=pltpu.CompilerParams(
            collective_id=0, has_side_effects=True, vmem_limit_bytes=60 * 2**20
        ),
    )(
        adjoint_prev, viscosity, friction, basal_velocity, ice_mask,
        misfit.reshape(2 * SB, TY), block_tile.reshape(1, SB), block_row.reshape(1, SB),
    )
    return pl.pallas_call(
        hand_on,
        out_shape=shapes,
        in_specs=[hbm] * 2,
        out_specs=(hbm, hbm),
        scratch_shapes=[pltpu.VMEM((2, LAYERS, TX, TY), F32), pltpu.VMEM((TX, TY), F32), dma((9,)), dma((9,))],
        compiler_params=pltpu.CompilerParams(vmem_limit_bytes=60 * 2**20),
    )(*results)


def solution(mesh):
    placed = (
        P(None, None, "gx", "gy"),
        P(None, "gx", "gy"),
        P("gx", "gy"),
        P(None, "gx", "gy"),
        P("gx", "gy"),
        P(("gx", "gy"), None, None),
        P(("gx", "gy"), None),
        P(("gx", "gy")),
    )
    return jax.shard_map(
        on_device,
        mesh=mesh,
        in_specs=placed,
        out_specs=(P(None, None, "gx", "gy"), P("gx", "gy")),
        check_vma=False,
    )
```

time: 64.5 us -> 43.8 us (0.68)
  the two profiles are of different devices: /device:TPU:1 before, /device:TPU:102 now
where the time goes in v2:
time: 43.8 us; the launch traced here: 43.6 us
  Pallas kernels  43 us (98%)
  between operations  0.64 us (1%)
    pallas_call x1, Pallas kernels, on_device(): pl.pallas_call(kernel, out_shape=shapes, in_specs=[hbm] * 8, out_specs=(h...  40.7 us
    pallas_call x1, Pallas kernels, on_device(): pl.pallas_call(hand_on, out_shape=shapes, in_specs=[hbm] * 2, out_specs=(...  2.23 us

profile of v2, /device:TPU:102, one launch (start us, length us, event | category | flops | bytes accessed | tf_op | source)
XLA Modules:
  0.0 43.6 jit_solution(12622234696190606179)
XLA Ops:
  0.6 40.7 %shard_map.95 = (f32[2,20,64,128]{3,2,1,0:T(8,128)}, f32[64,128]{1,0:T(8,128)}) custom-call(f32[2,20,64,128]{3,2,1,0:T(8,128)} %adj_hbm.1, f32[20,64,128]{2,1,0:T(8,128)} %eta_hbm.1, f32[64,128]{1,0:T(8,128)} %fric_hbm.1, f32[2,64,128]{2,1,0:T(8,128)} %vel_hbm.1, s32[64,128]{1,0:T(8,128)} %ice_hbm.1, bf16[2048,128]{1,0:T(8,128)(2,1)} %bitcast.3, ...), custom_call_target="tpu_custom_call" | custom-call | tf_op jit(solution)/shard_map/pallas_call | solution.py:655
  41.4 2.2 %shard_map.96 = (f32[2,20,64,128]{3,2,1,0:T(8,128)}, f32[64,128]{1,0:T(8,128)}) custom-call(f32[2,20,64,128]{3,2,1,0:T(8,128)} %get-tuple-element.4.adj_ref, f32[64,128]{1,0:T(8,128)} %get-tuple-element.5.grad_ref), custom_call_target="tpu_custom_call" | custom-call | tf_op jit(solution)/shard_map/pallas_call | solution.py:690

commit v3 on v2

--- a/solution.py
+++ b/solution.py
@@ -37,17 +37,17 @@
     return pltpu.roll(x, shift, 1)
 
 
-def four_n(e, f, o, heavy_x):
+def two_n(e, f, o, heavy_x):
     exm, exp_, eym, eyp = e
     fxm, fxp, fym, fyp = f
     dym, dyp, dxm, dxp = o
     if heavy_x:
-        x = exm * (4.0 * fxm - dym) + exp_ * (4.0 * fxp + dyp)
-        y = eym * (2.0 * fym - dxm) + eyp * (2.0 * fyp + dxp)
-        return 2.0 * x + y, 8.0 * (fxm + fxp), 2.0 * (fym + fyp)
-    x = exm * (2.0 * fxm - dym) + exp_ * (2.0 * fxp + dyp)
-    y = eym * (4.0 * fym - dxm) + eyp * (4.0 * fyp + dxp)
-    return x + 2.0 * y, 2.0 * (fxm + fxp), 8.0 * (fym + fyp)
+        fxm, fxp = 4.0 * fxm, 4.0 * fxp
+        total = exm * (fxm - dym) + exp_ * (fxp + dyp) + (eym * (fym - 0.5 * dxm) + eyp * (fyp + 0.5 * dxp))
+    else:
+        fym, fyp = 4.0 * fym, 4.0 * fyp
+        total = exm * (fxm - 0.5 * dym) + exp_ * (fxp + 0.5 * dyp) + (eym * (fym - dxm) + eyp * (fyp + dxp))
+    return total, (fxm + fxp) + (fym + fyp)
 
 
 def kernel(
@@ -204,12 +204,29 @@
     lax.fori_loop(0, GX, pack, 0)
 
     pl.semaphore_wait(bar2, GX - 1)
+    own_rows = pltpu.make_async_copy(rsend.at[me], rrecv.at[me], r_recv.at[0])
+    own_rows.start()
+
+    def send(j, carry):
+        px = lax.rem(me_x + j, GX)
+
+        def one(k, inner):
+            py = lax.rem(me_y + k, GY)
+            d = px * GY + py
+            pltpu.make_async_remote_copy(
+                rsend.at[d], rrecv.at[me], r_send, r_recv.at[j], device_id=(px, py), device_id_type=MESH
+            ).start()
+            return inner
+
+        lax.fori_loop(jnp.where(j == 0, 1, 0), GY, one, 0)
+        return carry
+
+    lax.fori_loop(0, GX, send, 0)
+
     own_values = pltpu.make_async_copy(sendb.at[me], recvb.at[me], a_recv.at[0])
-    own_rows = pltpu.make_async_copy(rsend.at[me], rrecv.at[me], r_recv.at[0])
     own_values.start()
-    own_rows.start()
-
-    def send(j, carry):
+
+    def send_values(j, carry):
         px = lax.rem(me_x + j, GX)
 
         def one(k, inner):
@@ -218,15 +235,12 @@
             pltpu.make_async_remote_copy(
                 sendb.at[d], recvb.at[me], a_send, a_recv.at[j], device_id=(px, py), device_id_type=MESH
             ).start()
-            pltpu.make_async_remote_copy(
-                rsend.at[d], rrecv.at[me], r_send, r_recv.at[j], device_id=(px, py), device_id_type=MESH
-            ).start()
             return inner
 
         lax.fori_loop(jnp.where(j == 0, 1, 0), GY, one, 0)
         return carry
 
-    lax.fori_loop(0, GX, send, 0)
+    lax.fori_loop(0, GX, send_values, 0)
 
     zero = jnp.zeros((8, 128), F32)
 
@@ -308,7 +322,7 @@
         du = 4.0 * dx4 + dy4 + rest
         dv = dx4 + 4.0 * dy4 + rest
         live = ice > 0.0
-        r = jnp.where(live, 0.25, 0.0) / jnp.where(live, du * dv, 1.0)
+        r = jnp.where(live, 0.5, 0.0) / jnp.where(live, du * dv, 1.0)
         return r * dv, r * du
 
     def neighbours(x, p):
@@ -394,8 +408,8 @@
                     diffs.append((mp - mm, pp - pm, pm - mm, pp - mp))
                 for c in range(2):
                     up, down = neighbours(mid[c], p)
-                    total, nx, ny = four_n(faces, own[c], diffs[1 - c], c == 0)
-                    total = total + e * (nx + ny + 8.0 * (up + down)) + 8.0 * (eu * up + ed * down)
+                    total, near = two_n(faces, own[c], diffs[1 - c], c == 0)
+                    total = total + e * (near + 4.0 * (up + down)) + 4.0 * (eu * up + ed * down)
                     new[c][p] = (1.0 - omega) * mid[c][p] + omega * (sg[c, p, w] * total)
                     dst[c, p, w] = new[c][p]
             for c in range(2):
@@ -424,8 +438,8 @@
                     diffs.append((mp - mm, pp - pm, pm - mm, pp - mp))
                 for c in range(2):
                     up, down = src[c, l, w], src[c, l + 2, w]
-                    total, nx, ny = four_n(faces, own[c], diffs[1 - c], c == 0)
-                    total = total + e * (nx + ny + 8.0 * (up + down)) + 8.0 * (eu * up + ed * down)
+                    total, near = two_n(faces, own[c], diffs[1 - c], c == 0)
+                    total = total + e * (near + 4.0 * (up + down)) + 4.0 * (eu * up + ed * down)
                     inv = (gu, gv)[c][l, w]
                     store(c, l, r, (1.0 - omega) * src[c, l + 1, w] + omega * (inv * total))
 
@@ -470,8 +484,8 @@
 
     for b in range(8):
         w = pl.ds(BASE + 8 * b, 8)
-        cu = (4.0 * omegas[0]) * (gu[0, w] * surf[pl.ds(8 * b, 8), pl.ds(0, 128)])
-        cv = (4.0 * omegas[0]) * (gv[0, w] * surf[pl.ds(8 * b, 8), pl.ds(128, 128)])
+        cu = (2.0 * omegas[0]) * (gu[0, w] * surf[pl.ds(8 * b, 8), pl.ds(0, 128)])
+        cv = (2.0 * omegas[0]) * (gv[0, w] * surf[pl.ds(8 * b, 8), pl.ds(128, 128)])
         c1[0, w] = cu
         c1[1, w] = cv
         ec[1, w] = jnp.where(lane < 8, roll(cu, 4), roll(cv, 12))
@@ -562,18 +576,12 @@
             mm, mp, pm, pp = tym[c, wm], typ[c, wm], tym[c, wp], typ[c, wp]
             diffs.append((mp - mm, pp - pm, pm - mm, pp - mp))
         for c in range(2):
-            total, nx, ny = four_n(faces, own[c], diffs[1 - c], c == 0)
-            tc2[0, c, w] = again1 * mid[c] + w1 * (tg[0, c, w] * (total + e * (nx + ny)))
-            tc2[1, c, w] = (8.0 * w1) * (tg[1, c, w] * ((e + te[1, w]) * mid[c]))
-
-    def shift_all(src, strip, slot):
-        for b in range(1, 11):
-            w = pl.ds(8 * b, 8)
-            for c in range(2):
-                t = strip(c, w)
-                ym, yp = shifted(src(c, w), jnp.where(right, roll(t, 124), roll(t, 60)))
-                ycm[slot, c, w] = ym
-                ycp[slot, c, w] = yp
+            total, near = two_n(faces, own[c], diffs[1 - c], c == 0)
+            for l, t in enumerate((
+                again1 * mid[c] + w1 * (tg[0, c, w] * (total + e * near)),
+                (4.0 * w1) * (tg[1, c, w] * ((e + te[1, w]) * mid[c])),
+            )):
+                tc2[l, c, w] = jnp.where(right, roll(t, 124), roll(t, 60))
 
     def around(src, slot, l, w, wm, wp):
         e = et[l + 1, w]
@@ -585,8 +593,8 @@
             diffs.append((mp - mm, pp - pm, pm - mm, pp - mp))
         sums = []
         for c in range(2):
-            total, nx, ny = four_n(faces, own[c], diffs[1 - c], c == 0)
-            sums.append(total + e * (nx + ny))
+            total, near = two_n(faces, own[c], diffs[1 - c], c == 0)
+            sums.append(total + e * near)
         return sums
 
     for r in starts:
@@ -595,17 +603,21 @@
         pair = et[1, w] + et[2, w]
         for c in range(2):
             z = c1[c, w]
-            c2[0, c, w] = again1 * z + w1 * ((gu, gv)[c][0, w] * sums[c])
-            c2[1, c, w] = (8.0 * w1) * ((gu, gv)[c][1, w] * (pair * z))
-    for l in range(2):
-        shift_all(lambda c, w: c2[l, c, w], lambda c, w: tc2[l, c, w], l)
+            for l, x in enumerate((
+                again1 * z + w1 * ((gu, gv)[c][0, w] * sums[c]),
+                (4.0 * w1) * ((gu, gv)[c][1, w] * (pair * z)),
+            )):
+                c2[l, c, w] = x
+                ym, yp = shifted(x, tc2[l, c, w])
+                ycm[1 + l, c, w] = ym
+                ycp[1 + l, c, w] = yp
     for b in range(8):
         r = BASE + 8 * b
         w, wm, wp = pl.ds(r, 8), pl.ds(r - 1, 8), pl.ds(r + 1, 8)
-        pair = 8.0 * (et[1, w] + et[2, w])
-        next_pair = (8.0 * w2) * (et[2, w] + et[3, w])
+        pair = 4.0 * (et[1, w] + et[2, w])
+        next_pair = (4.0 * w2) * (et[2, w] + et[3, w])
         for l in range(2):
-            sums = around(lambda c, x: c2[l, c, x], l, l, w, wm, wp)
+            sums = around(lambda c, x: c2[l, c, x], 1 + l, l, w, wm, wp)
             for c in range(2):
                 total = sums[c] + pair * c2[1 - l, c, w]
                 x = (1.0 - w2) * c2[l, c, w] + w2 * ((gu, gv)[c][l, w] * total)
@@ -675,7 +687,7 @@
             pltpu.VMEM((TX, 2 * TY), F32),
             padded(2), padded(2, 2), pltpu.VMEM((2, 3, TX, TY), F32),
             padded(3), padded(2), padded(2, 2), padded(2), padded(2),
-            padded(4), padded(2, 2), padded(2, 2), padded(2, 2),
+            padded(4), padded(2, 2), padded(3, 2), padded(3, 2),
             dma((8,)), dma, dma((GX,)), dma, dma((GX,)),
             dma((8,)), dma((8,)), dma((2,)), dma((2,)), dma((10,)), dma((10,)), dma((3,)),
             pltpu.SemaphoreType.REGULAR,

time: 43.8 us -> 40.2 us (0.918)
  the two profiles are of different devices: /device:TPU:102 before, /device:TPU:1 now
where the time goes in v3:
time: 40.2 us; the launch traced here: 39.6 us
  Pallas kernels  39 us (97%)
  between operations  0.64 us (2%)
    pallas_call x1, Pallas kernels, on_device(): pl.pallas_call(kernel, out_shape=shapes, in_specs=[hbm] * 8, out_specs=(h...  36.8 us
    pallas_call x1, Pallas kernels, on_device(): pl.pallas_call(hand_on, out_shape=shapes, in_specs=[hbm] * 2, out_specs=(...  2.23 us

profile of v3, /device:TPU:1, one launch (start us, length us, event | category | flops | bytes accessed | tf_op | source)
XLA Modules:
  0.0 39.6 jit_solution(288387798546090156)
XLA Ops:
  0.6 36.8 %shard_map.95 = (f32[2,20,64,128]{3,2,1,0:T(8,128)}, f32[64,128]{1,0:T(8,128)}) custom-call(f32[2,20,64,128]{3,2,1,0:T(8,128)} %adj_hbm.1, f32[20,64,128]{2,1,0:T(8,128)} %eta_hbm.1, f32[64,128]{1,0:T(8,128)} %fric_hbm.1, f32[2,64,128]{2,1,0:T(8,128)} %vel_hbm.1, s32[64,128]{1,0:T(8,128)} %ice_hbm.1, bf16[2048,128]{1,0:T(8,128)(2,1)} %bitcast.3, ...), custom_call_target="tpu_custom_call" | custom-call | tf_op jit(solution)/shard_map/pallas_call | solution.py:667
  37.4 2.2 %shard_map.96 = (f32[2,20,64,128]{3,2,1,0:T(8,128)}, f32[64,128]{1,0:T(8,128)}) custom-call(f32[2,20,64,128]{3,2,1,0:T(8,128)} %get-tuple-element.4.adj_ref, f32[64,128]{1,0:T(8,128)} %get-tuple-element.5.grad_ref), custom_call_target="tpu_custom_call" | custom-call | tf_op jit(solution)/shard_map/pallas_call | solution.py:702

commit v4 on v3

--- a/solution.py
+++ b/solution.py
@@ -66,6 +66,9 @@
 
     def at(dx, dy):
         return (lax.rem(me_x + dx + GX, GX), lax.rem(me_y + dy + GY, GY))
+
+    def alone(step):
+        lax.fori_loop(0, jnp.minimum(me_x, 0) + 1, lambda i, carry: (step(), carry)[1], 0)
 
     ins = [
         (tile_hbm, tile_v), (row_hbm, row_v), (mis_hbm, mis_v),
@@ -565,23 +568,26 @@
 
     w1, w2 = omegas[1], omegas[2]
     again1 = 1.0 - w1 + w1 / omegas[0]
-    for r in starts:
-        w, wm, wp = pl.ds(r, 8), pl.ds(r - 1, 8), pl.ds(r + 1, 8)
-        e = te[0, w]
-        faces = (te[0, wm], te[0, wp], te[2, w], te[3, w])
-        own, diffs, mid = [], [], []
-        for c in range(2):
-            mid.append(tc1[c, w])
-            own.append((tc1[c, wm], tc1[c, wp], tym[c, w], typ[c, w]))
-            mm, mp, pm, pp = tym[c, wm], typ[c, wm], tym[c, wp], typ[c, wp]
-            diffs.append((mp - mm, pp - pm, pm - mm, pp - mp))
-        for c in range(2):
-            total, near = two_n(faces, own[c], diffs[1 - c], c == 0)
-            for l, t in enumerate((
-                again1 * mid[c] + w1 * (tg[0, c, w] * (total + e * near)),
-                (4.0 * w1) * (tg[1, c, w] * ((e + te[1, w]) * mid[c])),
-            )):
-                tc2[l, c, w] = jnp.where(right, roll(t, 124), roll(t, 60))
+    def edge_strips():
+        for r in starts:
+            w, wm, wp = pl.ds(r, 8), pl.ds(r - 1, 8), pl.ds(r + 1, 8)
+            e = te[0, w]
+            faces = (te[0, wm], te[0, wp], te[2, w], te[3, w])
+            own, diffs, mid = [], [], []
+            for c in range(2):
+                mid.append(tc1[c, w])
+                own.append((tc1[c, wm], tc1[c, wp], tym[c, w], typ[c, w]))
+                mm, mp, pm, pp = tym[c, wm], typ[c, wm], tym[c, wp], typ[c, wp]
+                diffs.append((mp - mm, pp - pm, pm - mm, pp - mp))
+            for c in range(2):
+                total, near = two_n(faces, own[c], diffs[1 - c], c == 0)
+                for l, t in enumerate((
+                    again1 * mid[c] + w1 * (tg[0, c, w] * (total + e * near)),
+                    (4.0 * w1) * (tg[1, c, w] * ((e + te[1, w]) * mid[c])),
+                )):
+                    tc2[l, c, w] = jnp.where(right, roll(t, 124), roll(t, 60))
+
+    alone(edge_strips)
 
     def around(src, slot, l, w, wm, wp):
         e = et[l + 1, w]
@@ -597,36 +603,43 @@
             sums.append(total + e * near)
         return sums
 
-    for r in starts:
-        w, wm, wp = pl.ds(r, 8), pl.ds(r - 1, 8), pl.ds(r + 1, 8)
-        sums = around(lambda c, x: c1[c, x], 0, 0, w, wm, wp)
-        pair = et[1, w] + et[2, w]
-        for c in range(2):
-            z = c1[c, w]
-            for l, x in enumerate((
-                again1 * z + w1 * ((gu, gv)[c][0, w] * sums[c]),
-                (4.0 * w1) * ((gu, gv)[c][1, w] * (pair * z)),
-            )):
-                c2[l, c, w] = x
-                ym, yp = shifted(x, tc2[l, c, w])
-                ycm[1 + l, c, w] = ym
-                ycp[1 + l, c, w] = yp
-    for b in range(8):
-        r = BASE + 8 * b
-        w, wm, wp = pl.ds(r, 8), pl.ds(r - 1, 8), pl.ds(r + 1, 8)
-        pair = 4.0 * (et[1, w] + et[2, w])
-        next_pair = (4.0 * w2) * (et[2, w] + et[3, w])
-        for l in range(2):
-            sums = around(lambda c, x: c2[l, c, x], 1 + l, l, w, wm, wp)
+    def second():
+        for r in starts:
+            w, wm, wp = pl.ds(r, 8), pl.ds(r - 1, 8), pl.ds(r + 1, 8)
+            sums = around(lambda c, x: c1[c, x], 0, 0, w, wm, wp)
+            pair = et[1, w] + et[2, w]
             for c in range(2):
-                total = sums[c] + pair * c2[1 - l, c, w]
-                x = (1.0 - w2) * c2[l, c, w] + w2 * ((gu, gv)[c][l, w] * total)
-                if l == 0:
-                    x = x + (w2 / omegas[0]) * c1[c, w]
-                c3[c, l, pl.ds(8 * b, 8)] = fb[c, l + 1, w] + x
-        for c in range(2):
-            x = (gu, gv)[c][2, w] * (next_pair * c2[1, c, w])
-            c3[c, 2, pl.ds(8 * b, 8)] = fb[c, 3, w] + x
+                z = c1[c, w]
+                for l, x in enumerate((
+                    again1 * z + w1 * ((gu, gv)[c][0, w] * sums[c]),
+                    (4.0 * w1) * ((gu, gv)[c][1, w] * (pair * z)),
+                )):
+                    c2[l, c, w] = x
+                    ym, yp = shifted(x, tc2[l, c, w])
+                    ycm[1 + l, c, w] = ym
+                    ycp[1 + l, c, w] = yp
+
+    alone(second)
+
+    def third():
+        for b in range(8):
+            r = BASE + 8 * b
+            w, wm, wp = pl.ds(r, 8), pl.ds(r - 1, 8), pl.ds(r + 1, 8)
+            pair = 4.0 * (et[1, w] + et[2, w])
+            next_pair = (4.0 * w2) * (et[2, w] + et[3, w])
+            for l in range(2):
+                sums = around(lambda c, x: c2[l, c, x], 1 + l, l, w, wm, wp)
+                for c in range(2):
+                    total = sums[c] + pair * c2[1 - l, c, w]
+                    x = (1.0 - w2) * c2[l, c, w] + w2 * ((gu, gv)[c][l, w] * total)
+                    if l == 0:
+                        x = x + (w2 / omegas[0]) * c1[c, w]
+                    c3[c, l, pl.ds(8 * b, 8)] = fb[c, l + 1, w] + x
+            for c in range(2):
+                x = (gu, gv)[c][2, w] * (next_pair * c2[1, c, w])
+                c3[c, 2, pl.ds(8 * b, 8)] = fb[c, 3, w] + x
+
+    alone(third)
 
     out_high = pltpu.make_async_copy(c3, out_hbm.at[:, pl.ds(0, 3)], o_sem.at[1])
     out_high.start()

time: 40.2 us -> 39.6 us (0.985)
  Pallas kernels: 39 us -> 38.3 us
    pallas_call x1, Pallas kernels: 36.8 us -> 36.1 us  [on_device(): pl.pallas_call(kernel, out_shape=shapes, in_specs=[hbm] * 8, out_specs=(h...]
where the time goes in v4:
time: 39.6 us; the launch traced here: 39 us
  Pallas kernels  38.3 us (97%)
  between operations  0.64 us (2%)
    pallas_call x1, Pallas kernels, on_device(): pl.pallas_call(kernel, out_shape=shapes, in_specs=[hbm] * 8, out_specs=(h...  36.1 us
    pallas_call x1, Pallas kernels, on_device(): pl.pallas_call(hand_on, out_shape=shapes, in_specs=[hbm] * 2, out_specs=(...  2.23 us

profile of v4, /device:TPU:1, one launch (start us, length us, event | category | flops | bytes accessed | tf_op | source)
XLA Modules:
  0.0 39.0 jit_solution(7942553671243314321)
XLA Ops:
  0.6 36.1 %shard_map.95 = (f32[2,20,64,128]{3,2,1,0:T(8,128)}, f32[64,128]{1,0:T(8,128)}) custom-call(f32[2,20,64,128]{3,2,1,0:T(8,128)} %adj_hbm.1, f32[20,64,128]{2,1,0:T(8,128)} %eta_hbm.1, f32[64,128]{1,0:T(8,128)} %fric_hbm.1, f32[2,64,128]{2,1,0:T(8,128)} %vel_hbm.1, s32[64,128]{1,0:T(8,128)} %ice_hbm.1, bf16[2048,128]{1,0:T(8,128)(2,1)} %bitcast.3, ...), custom_call_target="tpu_custom_call" | custom-call | tf_op jit(solution)/shard_map/pallas_call | solution.py:680
  36.7 2.2 %shard_map.96 = (f32[2,20,64,128]{3,2,1,0:T(8,128)}, f32[64,128]{1,0:T(8,128)}) custom-call(f32[2,20,64,128]{3,2,1,0:T(8,128)} %get-tuple-element.4.adj_ref, f32[64,128]{1,0:T(8,128)} %get-tuple-element.5.grad_ref), custom_call_target="tpu_custom_call" | custom-call | tf_op jit(solution)/shard_map/pallas_call | solution.py:715
